TPU v7x, 32 devices: a whole 2x2x4 slice. The times are simulated.
32 devices in a mesh: ctx: 4 (over z), exp: 8 (over y, x, core).
Axes of the slice: x: 2, y: 2, z: 4, core: 2. Of those that a mesh axis runs over, the one named last changes fastest.
Arguments:
- tokens_in: bfloat16 [16, 1024, 768], P('exp', 'ctx'), may hold values from -6 to 6
- first_gain: bfloat16 [768], P('exp'), may hold values from 0.099609375 to 1.8984375
- joint_projection: bfloat16 [768, 2304], P('exp'), may hold values from -0.21875 to 0.21875
- out_projection: bfloat16 [768, 768], P('exp'), may hold values from -2.5 to 2.5
- bias_table: bfloat16 [32, 12], P('exp'), may hold values from -4 to 4
- second_gain: bfloat16 [768], P('exp'), may hold values from 0.099609375 to 1.8984375
- router_weight: bfloat16 [768, 8], P('exp'), may hold values from -0.15625 to 0.15625
- expert_up: bfloat16 [8, 768, 3072], P('exp', None, 'ctx'), may hold values from -0.21875 to 0.21875
- expert_down: bfloat16 [8, 3072, 768], P('exp', 'ctx'), may hold values from -0.95703125 to 0.95703125
- expert_index: int32 [16, 1024, 1], P('exp', 'ctx'), may hold values from 0 to 7; in each aligned block of 256 rows (0 to 255, 256 to 511, ..., all dimensions but the last counted through in order) at most 40 rows name the same one
- keep_mask: int32 [16, 1024], P('exp', 'ctx'), may hold values 0 or 1
- buckets: int32 [2047], replicated, may hold values from 0 to 31
- cotangent: bfloat16 [16, 1024, 768], P('exp', 'ctx'), may hold values from -6 to 6
Outputs:
- layer_out: bfloat16 [16, 1024, 768], P('exp', 'ctx')
- grad_tokens: float32 [16, 1024, 768], P('exp', 'ctx')
- grad_first_gain: float32 [768], P('exp')
- grad_joint: float32 [768, 2304], P('exp')
- grad_out_projection: float32 [768, 768], P('exp')
- grad_bias_table: float32 [32, 12], P('exp')
- grad_second_gain: float32 [768], P('exp')
- grad_router: float32 [768, 8], P('exp')
- grad_expert_up: float32 [8, 768, 3072], P('exp', None, 'ctx')
- grad_expert_down: float32 [8, 3072, 768], P('exp', 'ctx')
Inputs may be any that keep to these rules, and one draw needn't show every extreme that they name: `expert_index`: within each aligned block of 256 positions of a sequence, no expert is named by more than 40 tokens.
All inputs are finite; a program needn't handle non-finite values. No bound on the sum of `keep_mask` on one device may be relied on, other than what follows from the above.
Results may differ from a plain program's by a relative error of at most 0.02.
Values may be sent and summed in bfloat16 or wider, within the bound.
No kernel may reach another device: no remote copies, remote signals or barrier semaphores. Data moves between devices by JAX's collectives and lax.ppermute only.
A program may use at most 256 MiB of HBM per device.

v0:
```python
import functools

import jax
import jax.numpy as jnp
from jax import lax
from jax.experimental import pallas as pl
from jax.experimental.pallas import tpu as pltpu
from jax.sharding import PartitionSpec as P

EPSILON = 1e-06
HALF = 64
TILE = 128
GROUP = 256
VMEM_BYTES = 50 * 1024 * 1024
SCORE_SCALE = 0.125
HIGHEST = lax.Precision.HIGHEST
BOTH = ("ctx", "exp")


def contract_last(left, right):
    return lax.dot_general(
        left, right, (((1,), (1,)), ((), ())), preferred_element_type=jnp.float32
    )


def matmul(left, right):
    return lax.dot_general(
        left, right, (((1,), (0,)), ((), ())), preferred_element_type=jnp.float32
    )


def skew_kernel(offset_ref, skew_ref):
    padded = offset_ref.shape[-1]
    kept = skew_ref.shape[1]
    rows = jnp.broadcast_to(offset_ref[0], (TILE, padded))
    rolled = pltpu.roll(rows, padded - (TILE - 1), 1, stride=1, stride_axis=0)
    skew_ref[0] = rolled[:, :kept].T.astype(skew_ref.dtype)


def make_skew(offset_values):
    head_count, padded = offset_values.shape
    kept = padded - TILE
    return pl.pallas_call(
        skew_kernel,
        grid=(head_count,),
        in_specs=[pl.BlockSpec((1, 1, padded), lambda h: (h, 0, 0))],
        out_specs=pl.BlockSpec((1, kept, TILE), lambda h: (h, 0, 0)),
        out_shape=jax.ShapeDtypeStruct((head_count, kept, TILE), jnp.bfloat16),
        compiler_params=pltpu.CompilerParams(vmem_limit_bytes=VMEM_BYTES),
        name="skew_bias",
    )(offset_values.reshape(head_count, 1, padded))


def half_mask(rows, half):
    lanes = lax.broadcasted_iota(jnp.int32, (rows, TILE), 1)
    return (lanes // HALF) == half


def bias_rows(key_base, query_base, seq_len):
    return key_base - query_base + seq_len - TILE


def forward_kernel(
    base_ref, q_ref, k_ref, v_ref, skew_ref, out_ref, lse_ref, score_ref, prob_ref, *, chunk
):
    query_rows = q_ref.shape[0]
    key_rows = k_ref.shape[0]
    seq_len = key_rows
    mask = [half_mask(GROUP, 0), half_mask(GROUP, 1)]
    value_t = v_ref[...].T
    for group in range(query_rows // GROUP):
        rows = slice(group * GROUP, (group + 1) * GROUP)
        query_base = base_ref[0] + group * GROUP
        halves = []
        for half in range(2):
            queries = jnp.where(mask[half], q_ref[rows], 0).astype(jnp.bfloat16)
            score_ref[half] = contract_last(k_ref[...], queries)
            top = jnp.full((8, GROUP), -jnp.inf, jnp.float32)
            for start in range(0, key_rows, chunk):
                key_base = base_ref[start // query_rows] + start % query_rows
                place = pl.multiple_of(bias_rows(key_base, query_base, seq_len), TILE)
                left = skew_ref[half, pl.ds(place, chunk), :]
                right = skew_ref[half, pl.ds(place - TILE, chunk), :]
                bias = jnp.concatenate([left, right], axis=1).astype(jnp.float32)
                piece = score_ref[half, start : start + chunk] + bias
                score_ref[half, start : start + chunk] = piece
                top = jnp.maximum(top, jnp.max(piece.reshape(chunk // 8, 8, GROUP), axis=0))
            top = jnp.max(top, axis=0, keepdims=True)
            total = jnp.zeros((8, GROUP), jnp.float32)
            for start in range(0, key_rows, chunk):
                piece = jnp.exp(score_ref[half, start : start + chunk] - top)
                total = total + jnp.sum(piece.reshape(chunk // 8, 8, GROUP), axis=0)
                prob_ref[half, start : start + chunk] = piece.astype(jnp.bfloat16)
            total = jnp.sum(total, axis=0, keepdims=True)
            lse_ref[0, half : half + 1, rows] = top + jnp.log(total)
            mixed = matmul(value_t[half * HALF : (half + 1) * HALF], prob_ref[half])
            halves.append(mixed / total)
        out_ref[rows] = jnp.concatenate(halves, axis=0).T


def attend_forward(bases, queries, key_values, skew):
    query_rows, width = queries.shape
    key_rows = key_values.shape[0]
    kept = skew.shape[1]
    pairs = width // TILE
    chunk = TILE
    return pl.pallas_call(
        functools.partial(forward_kernel, chunk=chunk),
        grid_spec=pltpu.PrefetchScalarGridSpec(
            num_scalar_prefetch=1,
            grid=(pairs,),
            in_specs=[
                pl.BlockSpec((query_rows, TILE), lambda p, _: (0, p)),
                pl.BlockSpec((key_rows, TILE), lambda p, _: (0, p)),
                pl.BlockSpec((key_rows, TILE), lambda p, _: (0, p + pairs)),
                pl.BlockSpec((2, kept, TILE), lambda p, _: (p, 0, 0)),
            ],
            out_specs=[
                pl.BlockSpec((query_rows, TILE), lambda p, _: (0, p)),
                pl.BlockSpec((1, 2, query_rows), lambda p, _: (p, 0, 0)),
            ],
            scratch_shapes=[
                pltpu.VMEM((2, key_rows, GROUP), jnp.float32),
                pltpu.VMEM((2, key_rows, GROUP), jnp.bfloat16),
            ],
        ),
        out_shape=[
            jax.ShapeDtypeStruct((query_rows, width), jnp.float32),
            jax.ShapeDtypeStruct((pairs, 2, query_rows), jnp.float32),
        ],
        compiler_params=pltpu.CompilerParams(vmem_limit_bytes=VMEM_BYTES),
        name="attend_forward",
    )(bases, queries, key_values, key_values, skew)


def backward_kernel(
    base_ref, q_ref, do_ref, o_ref, k_ref, v_ref, skew_ref, lse_ref,
    dq_ref, dk_ref, dv_ref, off_ref,
    score_ref, gradp_ref, prob_ref, grads_ref, accum_k, accum_v, accum_skew,
    *, chunk,
):
    query_rows = q_ref.shape[0]
    key_rows = k_ref.shape[0]
    seq_len = key_rows
    mask = [half_mask(GROUP, 0), half_mask(GROUP, 1)]
    key_t = k_ref[...].T
    accum_skew[...] = jnp.zeros_like(accum_skew)
    for group in range(query_rows // GROUP):
        rows = slice(group * GROUP, (group + 1) * GROUP)
        query_base = base_ref[0] + group * GROUP
        product = (do_ref[rows].astype(jnp.float32) * o_ref[rows]).T
        halves = []
        sum_k = None
        for half in range(2):
            queries = jnp.where(mask[half], q_ref[rows], 0).astype(jnp.bfloat16)
            grads_out = jnp.where(mask[half], do_ref[rows], 0).astype(jnp.bfloat16)
            score_ref[half] = contract_last(k_ref[...], queries)
            gradp_ref[half] = contract_last(v_ref[...], grads_out)
            logsum = lse_ref[0, half : half + 1, rows]
            delta = jnp.sum(product[half * HALF : (half + 1) * HALF], axis=0, keepdims=True)
            for start in range(0, key_rows, chunk):
                key_base = base_ref[start // query_rows] + start % query_rows
                place = pl.multiple_of(bias_rows(key_base, query_base, seq_len), TILE)
                here = pl.ds(start, chunk)
                left = skew_ref[half, pl.ds(place, chunk), :]
                right = skew_ref[half, pl.ds(place - TILE, chunk), :]
                bias = jnp.concatenate([left, right], axis=1).astype(jnp.float32)
                prob = jnp.exp(score_ref[half, here] + bias - logsum)
                grads = prob * (gradp_ref[half, here] - delta)
                prob_ref[half, here] = prob.astype(jnp.bfloat16)
                grads_ref[half, here] = grads.astype(jnp.bfloat16)
                accum_skew[half, pl.ds(place, chunk), :] += grads[:, :TILE]
                accum_skew[half, pl.ds(place - TILE, chunk), :] += grads[:, TILE:]
            part_k = matmul(grads_ref[half], queries)
            part_v = matmul(prob_ref[half], grads_out)
            sum_k = part_k if sum_k is None else sum_k + part_k
            sum_v = part_v if half == 0 else sum_v + part_v
            halves.append(matmul(key_t[half * HALF : (half + 1) * HALF], grads_ref[half]))
        if group == 0:
            accum_k[...] = sum_k
            accum_v[...] = sum_v
        else:
            accum_k[...] += sum_k
            accum_v[...] += sum_v
        dq_ref[rows] = (jnp.concatenate(halves, axis=0) * 0.125).T.astype(dq_ref.dtype)
    dk_ref[...] = accum_k[...].astype(dk_ref.dtype)
    dv_ref[...] = accum_v[...].astype(dv_ref.dtype)
    for half in range(2):
        turned = accum_skew[half].T
        padded = turned.shape[1]
        count = TILE // 2
        while count:
            turned = turned[:count] + pltpu.roll(turned[count : 2 * count], padded - count, 1)
            count //= 2
        off_ref[0, half : half + 1] = pltpu.roll(turned, TILE - 1, 1)


def attend_backward(bases, queries, grads_out, outputs, key_values, skew, logsum):
    query_rows, width = queries.shape
    key_rows = key_values.shape[0]
    kept = skew.shape[1]
    pairs = width // TILE
    chunk = TILE
    column = lambda count: pl.BlockSpec((count, TILE), lambda p, _: (0, p))
    return pl.pallas_call(
        functools.partial(backward_kernel, chunk=chunk),
        grid_spec=pltpu.PrefetchScalarGridSpec(
            num_scalar_prefetch=1,
            grid=(pairs,),
            in_specs=[
                column(query_rows), column(query_rows), column(query_rows),
                column(key_rows),
                pl.BlockSpec((key_rows, TILE), lambda p, _: (0, p + pairs)),
                pl.BlockSpec((2, kept, TILE), lambda p, _: (p, 0, 0)),
                pl.BlockSpec((1, 2, query_rows), lambda p, _: (p, 0, 0)),
            ],
            out_specs=[
                column(query_rows), column(key_rows), column(key_rows),
                pl.BlockSpec((1, 2, kept + TILE), lambda p, _: (p, 0, 0)),
            ],
            scratch_shapes=[
                pltpu.VMEM((2, key_rows, GROUP), jnp.float32),
                pltpu.VMEM((2, key_rows, GROUP), jnp.float32),
                pltpu.VMEM((2, key_rows, GROUP), jnp.bfloat16),
                pltpu.VMEM((2, key_rows, GROUP), jnp.bfloat16),
                pltpu.VMEM((key_rows, TILE), jnp.float32),
                pltpu.VMEM((key_rows, TILE), jnp.float32),
                pltpu.VMEM((2, kept + TILE, TILE), jnp.float32),
            ],
        ),
        out_shape=[
            jax.ShapeDtypeStruct((query_rows, width), jnp.bfloat16),
            jax.ShapeDtypeStruct((key_rows, width), jnp.bfloat16),
            jax.ShapeDtypeStruct((key_rows, width), jnp.bfloat16),
            jax.ShapeDtypeStruct((pairs, 2, kept + TILE), jnp.float32),
        ],
        compiler_params=pltpu.CompilerParams(vmem_limit_bytes=VMEM_BYTES),
        name="attend_backward",
    )(bases, queries, grads_out, outputs, key_values, key_values, skew, logsum)


def rms_forward(row_data, gain_vec):
    inverse = lax.rsqrt(jnp.mean(row_data * row_data, axis=-1, keepdims=True) + EPSILON)
    return (row_data * inverse * gain_vec, inverse)


def rms_backward(row_data, inverse, gain_vec, grad_out):
    normed = row_data * inverse
    grad_gain = jnp.sum(grad_out * normed, axis=0)
    scaled = grad_out * gain_vec
    spread = jnp.mean(scaled * normed, axis=-1, keepdims=True)
    return (inverse * (scaled - normed * spread), grad_gain)


class Layout:
    def __init__(self):
        self.ctx_count = lax.axis_size("ctx")
        self.exp_count = lax.axis_size("exp")
        self.span = self.ctx_count // 4
        self.members = 2 * self.span
        self.ctx = lax.axis_index("ctx")
        self.core = lax.axis_index("exp") % 2
        self.member = (self.ctx % self.span) * 2 + self.core
        self.side = (self.ctx // self.span) % 2

    def number(self, ctx, exp):
        return ctx * self.exp_count + exp

    def round_pairs(self, turn):
        pairs = []
        for ctx in range(self.ctx_count):
            for exp in range(self.exp_count):
                seq = 2 * (exp % 2) + (turn + ctx) % 2
                member = ctx // 2
                target = self.number(seq * self.span + member // 2, exp // 2 * 2 + member % 2)
                pairs.append((self.number(ctx, exp), target))
        return pairs

    def member_pairs(self, shift):
        pairs = []
        for ctx in range(self.ctx_count):
            for exp in range(self.exp_count):
                start = ctx // self.span * self.span
                member = ((ctx - start) * 2 + exp % 2 + shift) % self.members
                target = self.number(start + member // 2, exp // 2 * 2 + member % 2)
                pairs.append((self.number(ctx, exp), target))
        return pairs

    def gather_blocks(self, blocks):
        got = [
            lax.ppermute(
                lax.dynamic_index_in_dim(blocks, (turn + self.ctx) % 2, 0, keepdims=False),
                BOTH,
                self.round_pairs(turn),
            )
            for turn in range(2)
        ]
        first = jnp.where(self.side == 0, got[0], got[1])
        second = jnp.where(self.side == 0, got[1], got[0])
        return jnp.concatenate([first, second], axis=0)

    def return_blocks(self, rows):
        blocks = rows.reshape((2, rows.shape[0] // 2) + rows.shape[1:])
        got = [
            lax.ppermute(
                lax.dynamic_index_in_dim(blocks, (turn + self.side) % 2, 0, keepdims=False),
                BOTH,
                [(target, source) for source, target in self.round_pairs(turn)],
            )
            for turn in range(2)
        ]
        even = self.ctx % 2 == 0
        return jnp.stack([jnp.where(even, got[0], got[1]), jnp.where(even, got[1], got[0])])

    def all_rows(self, rows):
        return jnp.concatenate(
            [rows]
            + [lax.ppermute(rows, BOTH, self.member_pairs(shift)) for shift in range(1, self.members)],
            axis=0,
        )

    def sum_rows(self, partial):
        parts = partial.reshape((self.members, partial.shape[0] // self.members) + partial.shape[1:])
        total = parts[0]
        for shift in range(1, self.members):
            moved = lax.ppermute(
                parts[shift].astype(jnp.bfloat16), BOTH, self.member_pairs(self.members - shift)
            )
            total = total + moved.astype(jnp.float32)
        return total

    def bases(self, row_count):
        return jnp.stack(
            [(self.member - shift) % self.members * row_count for shift in range(self.members)]
        ).astype(jnp.int32)

    def swap(self, rows, distance, axis="ctx"):
        pairs = [(place, place ^ distance) for place in range(lax.axis_size(axis))]
        return lax.ppermute(rows, axis, pairs)

    def gather_small(self, part):
        held = part[None]
        place = lax.axis_index("exp")
        distance = 1
        while distance < self.exp_count:
            other = self.swap(held, distance, "exp")
            upper = (place // distance) % 2 == 1
            held = jnp.where(
                upper,
                jnp.concatenate([other, held], axis=0),
                jnp.concatenate([held, other], axis=0),
            )
            distance *= 2
        return held

    def reduce_dense(self, part):
        rows = part.shape[0] // self.exp_count
        pair_count = self.exp_count // 2
        blocks = part.reshape(pair_count, 2, rows, part.shape[1])
        sent = lax.dynamic_index_in_dim(blocks, 1 - self.core, 1, keepdims=False)
        kept = lax.dynamic_index_in_dim(blocks, self.core, 1, keepdims=False)
        both = add_low([kept, self.swap(sent, 1, "exp")])
        pair = lax.axis_index("exp") // 2
        parts = [lax.dynamic_index_in_dim(both, pair, 0, keepdims=False)]
        for step in range(1, pair_count):
            block = lax.dynamic_index_in_dim(both, pair ^ step, 0, keepdims=False)
            parts.append(self.swap(block, 2 * step, "exp"))
        total = add_low(parts)
        cuts = total.reshape(self.ctx_count, rows // self.ctx_count, part.shape[1])
        parts = [lax.dynamic_index_in_dim(cuts, self.ctx, 0, keepdims=False)]
        for step in range(1, self.ctx_count):
            block = lax.dynamic_index_in_dim(cuts, self.ctx ^ step, 0, keepdims=False)
            parts.append(self.swap(block, step))
        own = add_low(parts)
        every = jnp.stack([own] + [self.swap(own, step) for step in range(1, self.ctx_count)])
        return jnp.concatenate(
            [
                lax.dynamic_index_in_dim(every, self.ctx ^ place, 0, keepdims=False)
                for place in range(self.ctx_count)
            ],
            axis=0,
        )


def add_low(parts):
    total = parts[0].astype(jnp.float32)
    for part in parts[1:]:
        total = total + part.astype(jnp.float32)
    return total.astype(jnp.bfloat16)


def after(value, *events):
    return lax.optimization_barrier((value,) + events)[0]


def per_device(
    tokens_in,
    first_gain,
    joint_projection,
    out_projection,
    bias_table,
    second_gain,
    router_weight,
    expert_up,
    expert_down,
    expert_index,
    keep_mask,
    buckets,
    cotangent,
):
    layout = Layout()
    shards = layout.exp_count
    seq_count, block_len, model_width = tokens_in.shape
    token_count = seq_count * block_len
    expert_count = router_weight.shape[1]
    bucket_count = bias_table.shape[0] * shards
    head_count = bias_table.shape[1]

    small = [first_gain, second_gain, router_weight, bias_table]
    small_sizes = [part.size for part in small]
    small_cuts = [sum(small_sizes[:place]) for place in range(1, len(small))]
    small_count = sum(small_sizes)
    small_padded = -(-small_count // TILE) * TILE
    small_full = layout.gather_small(
        jnp.pad(
            jnp.concatenate([part.reshape(-1) for part in small]), (0, small_padded - small_count)
        )
    )[:, :small_count]
    gain_one, gain_two, weight_router, table = jnp.split(small_full, small_cuts, axis=1)
    weight_router = weight_router.reshape(model_width, expert_count)
    table = table.reshape(bucket_count, head_count)
    gain_first = gain_one.reshape(model_width).astype(jnp.float32)
    gain_second = gain_two.reshape(model_width).astype(jnp.float32)
    weight_joint = lax.all_gather(joint_projection, "exp", axis=0, tiled=True)
    weight_out = lax.all_gather(out_projection, "exp", axis=0, tiled=True)

    tokens = layout.gather_blocks(tokens_in)
    codes = layout.gather_blocks(expert_index.reshape(seq_count, block_len) * 2 + keep_mask)
    grad_out_low = layout.gather_blocks(cotangent)
    every_token = layout.all_rows(tokens)
    chosen = codes // 2
    kept = codes % 2

    distances = list(range(2, layout.ctx_count, 2))
    up_moved = [layout.swap(expert_up[0], step) for step in distances]
    down_moved = [layout.swap(expert_down[0], step) for step in distances]

    offset_count = buckets.shape[0]
    bucket_hot = buckets[None, :] == jnp.arange(bucket_count, dtype=jnp.int32)[:, None]
    offset_values = lax.dot_general(
        table,
        bucket_hot.astype(jnp.bfloat16),
        (((0,), (0,)), ((), ())),
        preferred_element_type=jnp.float32,
    )
    skew = make_skew(jnp.pad(offset_values, ((0, 0), (0, 1))))

    is_choice = chosen[:, None] == jnp.arange(expert_count, dtype=jnp.int32)
    most_rows = max(2, (5 * block_len + 4 * expert_count - 1) // (4 * expert_count))
    capacity = seq_count * most_rows
    place = jnp.arange(token_count, dtype=jnp.int32)
    earlier = (place[:, None] >= place[None, :]) & (
        place[:, None] // block_len == place[None, :] // block_len
    )
    running = jnp.dot(
        earlier.astype(jnp.bfloat16),
        is_choice.astype(jnp.bfloat16),
        preferred_element_type=jnp.float32,
    )
    slot_rank = (jnp.sum(running * is_choice.astype(jnp.float32), axis=-1) - 1.0).astype(jnp.int32)
    token_slot = chosen * capacity + place // block_len * most_rows + slot_rank
    slot_hot = (
        (token_slot[:, None] == jnp.arange(expert_count * capacity, dtype=jnp.int32))
        & (kept[:, None] > 0)
    ).astype(jnp.bfloat16)

    def exchange(row_data):
        return lax.all_to_all(
            row_data.reshape(shards, -1, model_width), "exp", split_axis=0, concat_axis=0, tiled=True
        ).reshape(-1, model_width)

    def to_experts(row_data):
        sent = lax.dot_general(
            slot_hot, row_data, (((0,), (0,)), ((), ())), preferred_element_type=jnp.float32
        ).astype(jnp.bfloat16)
        return exchange(sent)

    def sum_halves(own_part, other_part):
        other = layout.swap(other_part, 1)
        return (own_part + other.astype(jnp.float32)).astype(jnp.bfloat16)

    def from_experts(summed):
        return jnp.dot(slot_hot, exchange(summed), preferred_element_type=jnp.float32)

    grad_own = to_experts(grad_out_low)
    grad_other = layout.swap(grad_own, 1)

    every_float = every_token.astype(jnp.float32)
    tokens_f = every_float[:token_count]
    normed_one, every_inverse = rms_forward(every_float, gain_first)
    inverse_one = every_inverse[:token_count]
    hidden_one = after(normed_one.astype(jnp.bfloat16), grad_out_low)
    queries = jnp.dot(
        hidden_one[:token_count], weight_joint[:, :model_width], preferred_element_type=jnp.float32
    ).astype(jnp.bfloat16) * jnp.bfloat16(SCORE_SCALE)
    key_values = jnp.dot(
        hidden_one, weight_joint[:, model_width:], preferred_element_type=jnp.float32
    ).astype(jnp.bfloat16)
    bases = layout.bases(token_count)
    attended, logsum = attend_forward(bases, queries, key_values, skew)
    attended = after(attended, grad_own)
    attended_low = attended.astype(jnp.bfloat16)
    residual = tokens_f + jnp.dot(attended_low, weight_out, preferred_element_type=jnp.float32)
    normed_two, inverse_two = rms_forward(residual, gain_second)
    hidden_two = normed_two.astype(jnp.bfloat16)

    row_own = after(to_experts(hidden_two), grad_other, *up_moved, *down_moved)
    row_other = layout.swap(row_own, 1)
    ups = [expert_up[0]] + up_moved
    downs = [expert_down[0]] + down_moved

    expert_here = jnp.arange(expert_count, dtype=jnp.int32) == lax.axis_index("exp")
    expert_here = expert_here.astype(jnp.float32)[None, :]

    def contract_rows(left, right):
        return lax.dot_general(
            left, right, (((0,), (0,)), ((), ())), preferred_element_type=jnp.float32
        )

    results, grad_inputs = [], []
    grad_router = 0.0
    grad_ups, grad_downs = [0.0] * len(ups), [0.0] * len(ups)
    for rows, grad_rows in ((row_own, grad_own), (row_other, grad_other)):
        logits = jnp.dot(rows, weight_router, preferred_element_type=jnp.float32)
        router_prob = jax.nn.softmax(logits, axis=-1)
        picked = jnp.sum(router_prob * expert_here, axis=-1, keepdims=True)
        grad_float = grad_rows.astype(jnp.float32)
        grad_result = (picked * grad_float).astype(jnp.bfloat16)
        produced, grad_input = 0.0, 0.0
        for part, (matrix_up, matrix_down) in enumerate(zip(ups, downs)):
            before = jnp.dot(rows, matrix_up, preferred_element_type=jnp.float32)
            activated, gelu_back = jax.vjp(jax.nn.gelu, before)
            acted = activated.astype(jnp.bfloat16)
            produced = produced + jnp.dot(acted, matrix_down, preferred_element_type=jnp.float32)
            grad_acted = contract_last(grad_result, matrix_down)
            grad_before = gelu_back(grad_acted)[0].astype(jnp.bfloat16)
            grad_input = grad_input + contract_last(grad_before, matrix_up)
            grad_ups[part] = grad_ups[part] + contract_rows(rows, grad_before)
            grad_downs[part] = grad_downs[part] + contract_rows(acted, grad_result)
        grad_picked = jnp.sum(grad_float * produced, axis=-1, keepdims=True)
        grad_logits = (picked * (expert_here - router_prob) * grad_picked).astype(jnp.bfloat16)
        grad_router = grad_router + contract_rows(rows, grad_logits)
        grad_inputs.append(grad_input + contract_last(grad_logits, weight_router))
        results.append(picked * produced)

    grad_summed = sum_halves(grad_inputs[0], grad_inputs[1].astype(jnp.bfloat16))
    grad_back = from_experts(grad_summed)
    result_other = after(results[1].astype(jnp.bfloat16), grad_summed)
    layer_rows = residual + from_experts(sum_halves(results[0], result_other))
    layer_out = layout.return_blocks(layer_rows.astype(jnp.bfloat16))

    down_low = [part.astype(jnp.bfloat16) for part in grad_downs[1:]]
    up_low = [part.astype(jnp.bfloat16) for part in grad_ups[1:]]

    def moved(parts):
        return [layout.swap(part, step) for part, step in zip(parts, distances)]

    grads_down_moved = moved(down_low)
    grads_up_moved = moved(up_low)

    def own_slice(own, others):
        total = own
        for other in others:
            total = total + other.astype(jnp.float32)
        return total[None]

    grad_residual, grad_gain_two = rms_backward(residual, inverse_two, gain_second, grad_back)
    grad_residual = grad_residual + grad_out_low.astype(jnp.float32)
    grad_mixed = grad_residual.astype(jnp.bfloat16)
    grad_weight_out = contract_rows(attended_low, grad_mixed)
    grad_attended = contract_last(grad_mixed, weight_out).astype(jnp.bfloat16)
    out_sum = layout.reduce_dense(grad_weight_out.astype(jnp.bfloat16))
    grad_q, grad_k, grad_v, grad_off = attend_backward(
        bases, queries, grad_attended, attended, key_values, skew, logsum
    )
    grad_k, *grads_down_moved = lax.optimization_barrier((grad_k, *grads_down_moved))
    grad_kv = jnp.concatenate([grad_k, grad_v], axis=1)
    partial_one = contract_last(grad_kv, weight_joint[:, model_width:])
    partial_own = contract_last(grad_q, weight_joint[:, :model_width])
    every_normed = every_float * every_inverse
    grad_gain_one = jnp.sum(partial_one * every_normed, axis=0) + jnp.sum(
        partial_own * every_normed[:token_count], axis=0
    )
    grad_hidden_one = layout.sum_rows(partial_one) + partial_own
    grad_input_norm, _ = rms_backward(tokens_f, inverse_one, gain_first, grad_hidden_one)
    grad_tokens = layout.return_blocks((grad_input_norm + grad_residual).astype(jnp.bfloat16)).astype(
        jnp.float32
    )
    kv_sum = layout.reduce_dense(contract_rows(hidden_one, grad_kv).astype(jnp.bfloat16))
    query_part = contract_rows(hidden_one[:token_count], grad_q).astype(jnp.bfloat16)
    query_part, *grads_up_moved = lax.optimization_barrier((query_part, *grads_up_moved))
    grad_expert_up = own_slice(grad_ups[0], grads_up_moved)
    grad_expert_down = own_slice(grad_downs[0], grads_down_moved)
    grad_table = jnp.dot(
        bucket_hot.astype(jnp.float32),
        grad_off.reshape(head_count, -1)[:, :offset_count].T,
        precision=HIGHEST,
    )
    small_grads = [grad_gain_one, grad_gain_two, grad_router, grad_table]
    shard_rows = joint_projection.shape[0]
    side_width = -(-small_count // (shard_rows * TILE)) * TILE
    small_grads = jnp.concatenate([part.reshape(shards, -1) for part in small_grads], axis=1)
    small_grads = jnp.pad(small_grads, ((0, 0), (0, shard_rows * side_width - small_count)))
    side = small_grads.reshape(shards * shard_rows, side_width).astype(jnp.bfloat16)
    query_sum = layout.reduce_dense(jnp.concatenate([query_part, side], axis=1))
    side_sum = query_sum[:, model_width:].reshape(-1)[:small_count].astype(jnp.float32)
    joint_sum = jnp.concatenate([query_sum[:, :model_width], kv_sum], axis=1)
    sum_gain_one, sum_gain_two, sum_router, sum_table = jnp.split(side_sum, small_cuts)
    return (
        layer_out,
        grad_tokens,
        sum_gain_one,
        joint_sum.astype(jnp.float32),
        out_sum.astype(jnp.float32),
        sum_table.reshape(bias_table.shape),
        sum_gain_two,
        sum_router.reshape(router_weight.shape),
        grad_expert_up,
        grad_expert_down,
    )


def solution(mesh):
    in_specs = (
        P("exp", "ctx", None),
        P("exp"),
        P("exp", None),
        P("exp", None),
        P("exp", None),
        P("exp"),
        P("exp", None),
        P("exp", None, "ctx"),
        P("exp", "ctx", None),
        P("exp", "ctx", None),
        P("exp", "ctx"),
        P(),
        P("exp", "ctx", None),
    )
    out_specs = (
        P("exp", "ctx", None),
        P("exp", "ctx", None),
        P("exp"),
        P("exp", None),
        P("exp", None),
        P("exp", None),
        P("exp"),
        P("exp", None),
        P("exp", None, "ctx"),
        P("exp", "ctx", None),
    )
    return jax.shard_map(
        per_device, mesh=mesh, in_specs=in_specs, out_specs=out_specs, check_vma=False
    )
```

profile of v0, /device:TPU:0, one launch (start us, length us, event | category | flops | bytes accessed | tf_op | source)
XLA Modules:
  0.0 498.7 jit_solution(14151180267295160901)
XLA Ops:
  31.3 17.3 %collective-permute-start.11 = (bf16[768,768]{1,0:T(8,128)(2,1)}, bf16[768,768]{1,0:T(8,128)(2,1)}, u32[]{:S(2)}, u32[]{:S(2)}) collective-permute-start(bf16[768,768]{1,0:T(8,128)(2,1)} %bitcast.272), channel_id=1, source_target_pairs={{0,16},{8,24},{16,0},{24,8},{1,17},{9,25},{17,1},{25,9},{2,18},{10... | collective-permute-start | bytes 3538952 | tf_op jit(solution)/shard_map/ppermute | solution.py:339
  53.0 59.7 %all-to-all-start = ((bf16[8,80,768]{2,1,0:T(8,128)(2,1)}), bf16[8,80,768]{2,1,0:T(8,128)(2,1)S(1)}, u32[]{:S(2)}, u32[]{:S(2)}) async-start(bf16[8,80,768]{2,1,0:T(8,128)(2,1)} %bitcast.252), calls=%async_computation | async-start | bytes 1966080 | tf_op jit(solution)/shard_map/all_to_all | solution.py:478
  112.9 7.4 %skew_bias.1.skew_ref = bf16[12,1920,128]{2,1,0:T(8,128)(2,1)} custom-call(f32[12,1,2048]{2,1,0:T(1,128)S(1)} %reshape.445.offset_ref), custom_call_target="tpu_custom_call" | custom-call | tf_op jit(solution)/shard_map/skew_bias/pallas_call | solution.py:43
  127.4 9.0 %collective-permute-start.10 = (bf16[640,768]{1,0:T(8,128)(2,1)S(1)}, bf16[640,768]{1,0:T(8,128)(2,1)}, u32[]{:S(2)}, u32[]{:S(2)}) collective-permute-start(bf16[640,768]{1,0:T(8,128)(2,1)S(1)} %bitcast.243), channel_id=1, source_target_pairs={{0,8},{8,0},{16,24},{24,16},{1,9},{9,1},{17,25},{25,17},{2,10},{10... | collective-permute-start | bytes 2949128 | tf_op jit(solution)/shard_map/ppermute | solution.py:339
  138.7 5.6 %convolution_convert_fusion.k_ref.v_ref = bf16[1024,1536]{1,0:T(8,128)(2,1)} fusion(bf16[1024,768]{1,0:T(8,128)(2,1)S(1)} %copy-done.28, bf16[768,2304]{1,0:T(8,128)(2,1)} %all-gather.3.cloned.1.call-done), kind=kOutput, calls=%fused_computation | convolution fusion | flops 2417491968 | bytes 7077888 | tf_op jit(solution)/shard_map/dot_general | solution.py:506
  144.3 20.7 %attend_forward.1 = (f32[512,768]{1,0:T(8,128)S(1)}, f32[6,2,512]{2,1,0:T(2,128)S(1)}) custom-call(s32[2]{0:T(128)S(1)} %pad_add_fusion.1.base_ref, bf16[512,768]{1,0:T(8,128)(2,1)S(1)} %fusion.46.q_ref, bf16[1024,1536]{1,0:T(8,128)(2,1)} %convolution_convert_fusion.k_ref.v_ref, bf16[1024,1536]{1,0:T(8,128)(2,1)} %convolution_convert_fusion.k_ref.v_ref, ...), custom_call_target="tpu_custom_call" | custom-call | tf_op jit(solution)/shard_map/attend_forward/pallas_call | solution.py:107
  171.3 3.8 all-to-all-start.1
  178.6 10.9 %all-to-all-done.1 = bf16[8,80,768]{2,1,0:T(8,128)(2,1)S(1)} async-done(((bf16[8,80,768]{2,1,0:T(8,128)(2,1)}), bf16[8,80,768]{2,1,0:T(8,128)(2,1)S(1)}, u32[]{:S(2)}, u32[]{:S(2)}) %all-to-all-start.1) | async-done | bytes 983072 | tf_op jit(solution)/shard_map/all_to_all | solution.py:478
  192.3 4.2 fusion.162
  199.1 11.1 %collective-permute-done.13 = bf16[640,768]{1,0:T(8,128)(2,1)S(1)} collective-permute-done((bf16[640,768]{1,0:T(8,128)(2,1)S(1)}, bf16[640,768]{1,0:T(8,128)(2,1)S(1)}, u32[]{:S(2)}, u32[]{:S(2)}) %collective-permute-start.13) | collective-permute-done | bytes 983072 | tf_op jit(solution)/shard_map/ppermute | solution.py:339
  211.7 5.4 %fusion.4 = (bf16[640,768]{1,0:T(8,128)(2,1)S(1)}, f32[640]{0:T(1024)S(1)}, f32[640,768]{1,0:T(8,128)}) fusion(f32[640]{0:T(1024)S(1)} %get-tuple-element.52, bf16[8,80,768]{2,1,0:T(8,128)(2,1)S(1)} %all-to-all-done, f32[640,768]{1,0:T(8,128)} %fusion.135, bf16[768,768]{1,0:T(8,128)(2,1)} %collective-permute-done.12, f32[640,768]{1,0:T(8,128)} %fusion.162), kind=kOutput, calls=%fused_computation.26 | convolution fusion | flops 762346880 | bytes 9049088 | tf_op jit(solution)/shard_map/dot_general | solution.py:544
  220.8 3.9 add_convert_fusion.1
  230.6 4.0 fusion.7
  260.5 25.6 %collective-permute-done.14 = bf16[640,768]{1,0:T(8,128)(2,1)S(1)} collective-permute-done((bf16[640,768]{1,0:T(8,128)(2,1)S(1)}, bf16[640,768]{1,0:T(8,128)(2,1)S(1)}, u32[]{:S(2)}, u32[]{:S(2)}) %collective-permute-start.14) | collective-permute-done | bytes 983072 | tf_op jit(solution)/shard_map/ppermute | solution.py:339
  289.4 8.0 %all-to-all-start.3 = ((bf16[8,80,768]{2,1,0:T(8,128)(2,1)}), bf16[8,80,768]{2,1,0:T(8,128)(2,1)S(1)}, u32[]{:S(2)}, u32[]{:S(2)}) async-start(bf16[8,80,768]{2,1,0:T(8,128)(2,1)} %bitcast.23), calls=%async_computation.3 | async-start | bytes 1966080 | tf_op jit(solution)/shard_map/all_to_all | solution.py:478
  298.1 4.7 fusion.149
  302.8 4.2 fusion.151
  307.0 5.1 %all-to-all-done.3 = bf16[8,80,768]{2,1,0:T(8,128)(2,1)S(1)} async-done(((bf16[8,80,768]{2,1,0:T(8,128)(2,1)}), bf16[8,80,768]{2,1,0:T(8,128)(2,1)S(1)}, u32[]{:S(2)}, u32[]{:S(2)}) %all-to-all-start.3) | async-done | bytes 983072 | tf_op jit(solution)/shard_map/all_to_all | solution.py:478
  315.9 27.3 %attend_backward.1 = (bf16[512,768]{1,0:T(8,128)(2,1)S(1)}, bf16[1024,768]{1,0:T(8,128)(2,1)S(1)}, bf16[1024,768]{1,0:T(8,128)(2,1)}, f32[6,2,2048]{2,1,0:T(2,128)S(1)}) custom-call(s32[2]{0:T(128)S(1)} %pad_add_fusion.1.base_ref, bf16[512,768]{1,0:T(8,128)(2,1)S(1)} %fusion.46.q_ref, bf16[512,768]{1,0:T(8,128)(2,1)S(1)} %convolution_convert_fusion.6.do_ref, ...), custom_call_target="tpu_custom_call" | custom-call | tf_op jit(solution)/shard_map/attend_backward/pallas_call | solution.py:205
  356.3 4.3 multiply_reduce_fusion
  390.1 4.2 all-to-all-start.2
  399.7 5.2 %fusion.36 = (f32[768]{0:T(1024)S(1)}, f32[512]{0:T(512)S(1)}, f32[512,768]{1,0:T(8,128)}) fusion(f32[1024,768]{1,0:T(8,128)} %get-tuple-element.57, f32[512]{0:T(512)S(1)} %slice.64, f32[1024,768]{1,0:T(8,128)} %maximum_convert_fusion, f32[768]{0:T(1024)S(1)} %reshape.468, bf16[512,768]{1,0:T(8,128)(2,1)S(1)} %collective-permute-done.19, ...), kind=kOutput, calls=%fused_computation.70 | convolution fusion | flops 607517440 | bytes 9054208 | tf_op jit(solution)/shard_map/dot_general | solution.py:21
  425.9 7.2 %collective-permute-done.17 = bf16[256,768]{1,0:T(8,128)(2,1)S(1)} collective-permute-done((bf16[256,768]{1,0:T(8,128)(2,1)S(1)}, bf16[256,768]{1,0:T(8,128)(2,1)S(1)}, u32[]{:S(2)}, u32[]{:S(2)}) %collective-permute-start.17) | collective-permute-done | bytes 393248 | tf_op jit(solution)/shard_map/ppermute | solution.py:305
  436.3 20.8 %collective-permute-start.38 = (bf16[24,1536]{1,0:T(8,128)(2,1)S(1)}, bf16[24,1536]{1,0:T(8,128)(2,1)S(1)}, u32[]{:S(2)}, u32[]{:S(2)}) collective-permute-start(bf16[24,1536]{1,0:T(8,128)(2,1)S(1)} %get-tuple-element.91), channel_id=1, source_target_pairs={{0,16},{8,24},{16,0},{24,8},{1,17},{9,25},{17,1},{25,9},{2,18},{10... | collective-permute-start | bytes 221192 | tf_op jit(solution)/shard_map/ppermute | solution.py:339
  (358 shorter events, 203.3 us)
Async XLA Ops:
  7.2 129.1 %all-gather.3.cloned.1.call-start = ((), (), s32[]{:S(2)}) async-start(), calls=%async_computation.4 | async-start | bytes 3981312 | tf_op jit(solution)/shard_map/all_gather | solution.py:434
  8.0 157.0 %all-gather.5.cloned.1.call-start = ((), (), s32[]{:S(2)}) async-start(), calls=%async_computation.5 | async-start | bytes 1327104 | tf_op jit(solution)/shard_map/all_gather | solution.py:435
  9.2 39.5 %collective-permute-start = (bf16[256,768]{1,0:T(8,128)(2,1)S(1)}, bf16[256,768]{1,0:T(8,128)(2,1)S(1)}, u32[]{:S(2)}, u32[]{:S(2)}) collective-permute-start(bf16[256,768]{1,0:T(8,128)(2,1)S(1)} %get-tuple-element.77), channel_id=1, source_target_pairs={{0,0},{1,16},{2,2},{3,18},{4,4},{5,20},{6,6},{7,22},{8,8},{9,24},{... | collective-permute-start | bytes 1179656 | tf_op jit(solution)/shard_map/ppermute | solution.py:291
  9.9 38.9 %collective-permute-start.1 = (bf16[256,768]{1,0:T(8,128)(2,1)S(1)}, bf16[256,768]{1,0:T(8,128)(2,1)S(1)}, u32[]{:S(2)}, u32[]{:S(2)}) collective-permute-start(bf16[256,768]{1,0:T(8,128)(2,1)S(1)} %get-tuple-element.78), channel_id=1, source_target_pairs={{0,8},{1,24},{2,10},{3,26},{4,12},{5,28},{6,14},{7,30},{8,0},{9,16... | collective-permute-start | bytes 1179656 | tf_op jit(solution)/shard_map/ppermute | solution.py:291
  18.5 30.7 %collective-permute-start.6 = (bf16[256,768]{1,0:T(8,128)(2,1)S(1)}, bf16[256,768]{1,0:T(8,128)(2,1)}, u32[]{:S(2)}, u32[]{:S(2)}) collective-permute-start(bf16[256,768]{1,0:T(8,128)(2,1)S(1)} %get-tuple-element.73), channel_id=1, source_target_pairs={{0,0},{1,16},{2,2},{3,18},{4,4},{5,20},{6,6},{7,22},{8,8},{9,24},{... | collective-permute-start | bytes 1179656 | tf_op jit(solution)/shard_map/ppermute | solution.py:291
  21.9 27.4 %collective-permute-start.7 = (bf16[256,768]{1,0:T(8,128)(2,1)S(1)}, bf16[256,768]{1,0:T(8,128)(2,1)}, u32[]{:S(2)}, u32[]{:S(2)}) collective-permute-start(bf16[256,768]{1,0:T(8,128)(2,1)S(1)} %get-tuple-element.74), channel_id=1, source_target_pairs={{0,8},{1,24},{2,10},{3,26},{4,12},{5,28},{6,14},{7,30},{8,0},{9,16... | collective-permute-start | bytes 1179656 | tf_op jit(solution)/shard_map/ppermute | solution.py:291
  31.3 144.3 %collective-permute-start.11 = (bf16[768,768]{1,0:T(8,128)(2,1)}, bf16[768,768]{1,0:T(8,128)(2,1)}, u32[]{:S(2)}, u32[]{:S(2)}) collective-permute-start(bf16[768,768]{1,0:T(8,128)(2,1)} %bitcast.272), channel_id=1, source_target_pairs={{0,16},{8,24},{16,0},{24,8},{1,17},{9,25},{17,1},{25,9},{2,18},{10... | collective-permute-start | bytes 3538952 | tf_op jit(solution)/shard_map/ppermute | solution.py:339
  48.8 126.8 %collective-permute-start.12 = (bf16[768,768]{1,0:T(8,128)(2,1)}, bf16[768,768]{1,0:T(8,128)(2,1)}, u32[]{:S(2)}, u32[]{:S(2)}) collective-permute-start(bf16[768,768]{1,0:T(8,128)(2,1)} %bitcast.271), channel_id=1, source_target_pairs={{0,16},{8,24},{16,0},{24,8},{1,17},{9,25},{17,1},{25,9},{2,18},{10... | collective-permute-start | bytes 3538952 | tf_op jit(solution)/shard_map/ppermute | solution.py:339
  49.0 71.4 %collective-permute-start.2 = (bf16[512,768]{1,0:T(8,128)(2,1)S(1)}, bf16[512,768]{1,0:T(8,128)(2,1)S(1)}, u32[]{:S(2)}, u32[]{:S(2)}) collective-permute-start(bf16[512,768]{1,0:T(8,128)(2,1)S(1)} %pad_maximum_fusion.1), channel_id=1, source_target_pairs={{0,1},{1,0},{2,3},{3,2},{4,5},{5,4},{6,7},{7,6},{8,9},{9,8},{10,11... | collective-permute-start | bytes 2359304 | tf_op jit(solution)/shard_map/ppermute | solution.py:318
  53.0 74.4 %all-to-all-start = ((bf16[8,80,768]{2,1,0:T(8,128)(2,1)}), bf16[8,80,768]{2,1,0:T(8,128)(2,1)S(1)}, u32[]{:S(2)}, u32[]{:S(2)}) async-start(bf16[8,80,768]{2,1,0:T(8,128)(2,1)} %bitcast.252), calls=%async_computation | async-start | bytes 1966080 | tf_op jit(solution)/shard_map/all_to_all | solution.py:478
  127.4 51.2 %collective-permute-start.10 = (bf16[640,768]{1,0:T(8,128)(2,1)S(1)}, bf16[640,768]{1,0:T(8,128)(2,1)}, u32[]{:S(2)}, u32[]{:S(2)}) collective-permute-start(bf16[640,768]{1,0:T(8,128)(2,1)S(1)} %bitcast.243), channel_id=1, source_target_pairs={{0,8},{8,0},{16,24},{24,16},{1,9},{9,1},{17,25},{25,17},{2,10},{10... | collective-permute-start | bytes 2949128 | tf_op jit(solution)/shard_map/ppermute | solution.py:339
  189.5 20.6 %collective-permute-start.13 = (bf16[640,768]{1,0:T(8,128)(2,1)S(1)}, bf16[640,768]{1,0:T(8,128)(2,1)S(1)}, u32[]{:S(2)}, u32[]{:S(2)}) collective-permute-start(bf16[640,768]{1,0:T(8,128)(2,1)S(1)} %bitcast.232), channel_id=1, source_target_pairs={{0,8},{8,0},{16,24},{24,16},{1,9},{9,1},{17,25},{25,17},{2,10},{10... | collective-permute-start | bytes 2949128 | tf_op jit(solution)/shard_map/ppermute | solution.py:339
  224.7 119.3 %collective-permute-start.18 = (bf16[768,768]{1,0:T(8,128)(2,1)}, bf16[768,768]{1,0:T(8,128)(2,1)}, u32[]{:S(2)}, u32[]{:S(2)}) collective-permute-start(bf16[768,768]{1,0:T(8,128)(2,1)} %add_convert_fusion.1), channel_id=1, source_target_pairs={{0,16},{8,24},{16,0},{24,8},{1,17},{9,25},{17,1},{25,9},{2,18},{10... | collective-permute-start | bytes 3538952 | tf_op jit(solution)/shard_map/ppermute | solution.py:339
  245.3 40.8 %collective-permute-start.14 = (bf16[640,768]{1,0:T(8,128)(2,1)S(1)}, bf16[640,768]{1,0:T(8,128)(2,1)S(1)}, u32[]{:S(2)}, u32[]{:S(2)}) collective-permute-start(bf16[640,768]{1,0:T(8,128)(2,1)S(1)} %add_convert_fusion.4), channel_id=1, source_target_pairs={{0,8},{8,0},{16,24},{24,16},{1,9},{9,1},{17,25},{25,17},{2,10},{10... | collective-permute-start | bytes 2949128 | tf_op jit(solution)/shard_map/ppermute | solution.py:339
  252.3 110.2 %collective-permute-start.22 = (bf16[768,768]{1,0:T(8,128)(2,1)}, bf16[768,768]{1,0:T(8,128)(2,1)}, u32[]{:S(2)}, u32[]{:S(2)}) collective-permute-start(bf16[768,768]{1,0:T(8,128)(2,1)} %add_convert_fusion), channel_id=1, source_target_pairs={{0,16},{8,24},{16,0},{24,8},{1,17},{9,25},{17,1},{25,9},{2,18},{10... | collective-permute-start | bytes 3538952 | tf_op jit(solution)/shard_map/ppermute | solution.py:339
  289.4 22.8 %all-to-all-start.3 = ((bf16[8,80,768]{2,1,0:T(8,128)(2,1)}), bf16[8,80,768]{2,1,0:T(8,128)(2,1)S(1)}, u32[]{:S(2)}, u32[]{:S(2)}) async-start(bf16[8,80,768]{2,1,0:T(8,128)(2,1)} %bitcast.23), calls=%async_computation.3 | async-start | bytes 1966080 | tf_op jit(solution)/shard_map/all_to_all | solution.py:478
  307.0 77.7 %collective-permute-start.15 = (bf16[640,768]{1,0:T(8,128)(2,1)}, bf16[640,768]{1,0:T(8,128)(2,1)}, u32[]{:S(2)}, u32[]{:S(2)}) collective-permute-start(bf16[640,768]{1,0:T(8,128)(2,1)} %get-tuple-element.28), channel_id=1, source_target_pairs={{0,8},{8,0},{16,24},{24,16},{1,9},{9,1},{17,25},{25,17},{2,10},{10... | collective-permute-start | bytes 2949128 | tf_op jit(solution)/shard_map/ppermute | solution.py:339
  344.9 23.0 %collective-permute-start.43 = (bf16[4,96,768]{2,1,0:T(8,128)(2,1)}, bf16[4,96,768]{2,1,0:T(8,128)(2,1)}, u32[]{:S(2)}, u32[]{:S(2)}) collective-permute-start(bf16[4,96,768]{2,1,0:T(8,128)(2,1)} %dynamic-slice_bitcast_fusion.2), channel_id=1, source_target_pairs={{0,1},{1,0},{2,3},{3,2},{4,5},{5,4},{6,7},{7,6},{8,9},{9,8},{10,11... | collective-permute-start | bytes 1769480 | tf_op jit(solution)/shard_map/ppermute | solution.py:339
  350.9 66.7 %collective-permute-start.33 = (bf16[4,96,1536]{2,1,0:T(8,128)(2,1)}, bf16[4,96,1536]{2,1,0:T(8,128)(2,1)}, u32[]{:S(2)}, u32[]{:S(2)}) collective-permute-start(bf16[4,96,1536]{2,1,0:T(8,128)(2,1)} %dynamic-slice_bitcast_fusion), channel_id=1, source_target_pairs={{0,1},{1,0},{2,3},{3,2},{4,5},{5,4},{6,7},{7,6},{8,9},{9,8},{10,11... | collective-permute-start | bytes 3538952 | tf_op jit(solution)/shard_map/ppermute | solution.py:339
  377.7 22.0 %collective-permute-start.19 = (bf16[512,768]{1,0:T(8,128)(2,1)}, bf16[512,768]{1,0:T(8,128)(2,1)S(1)}, u32[]{:S(2)}, u32[]{:S(2)}) collective-permute-start(bf16[512,768]{1,0:T(8,128)(2,1)} %slice.116), channel_id=1, source_target_pairs={{0,1},{1,0},{2,3},{3,2},{4,5},{5,4},{6,7},{7,6},{8,9},{9,8},{10,11... | collective-permute-start | bytes 2359304 | tf_op jit(solution)/shard_map/ppermute | solution.py:326
  390.1 24.3 %all-to-all-start.2 = ((bf16[8,80,768]{2,1,0:T(8,128)(2,1)}), bf16[8,80,768]{2,1,0:T(8,128)(2,1)}, u32[]{:S(2)}, u32[]{:S(2)}) async-start(bf16[8,80,768]{2,1,0:T(8,128)(2,1)} %bitcast.244), calls=%async_computation.2 | async-start | bytes 1966080 | tf_op jit(solution)/shard_map/all_to_all | solution.py:478
  409.5 47.6 %collective-permute-start.23 = (bf16[4,96,896]{2,1,0:T(8,128)(2,1)}, bf16[4,96,896]{2,1,0:T(8,128)(2,1)}, u32[]{:S(2)}, u32[]{:S(2)}) collective-permute-start(bf16[4,96,896]{2,1,0:T(8,128)(2,1)} %dynamic-slice_bitcast_fusion.1), channel_id=1, source_target_pairs={{0,1},{1,0},{2,3},{3,2},{4,5},{5,4},{6,7},{7,6},{8,9},{9,8},{10,11... | collective-permute-start | bytes 2064392 | tf_op jit(solution)/shard_map/ppermute | solution.py:339
  435.7 26.2 %collective-permute-start.37 = (bf16[24,1536]{1,0:T(8,128)(2,1)S(1)}, bf16[24,1536]{1,0:T(8,128)(2,1)S(1)}, u32[]{:S(2)}, u32[]{:S(2)}) collective-permute-start(bf16[24,1536]{1,0:T(8,128)(2,1)S(1)} %get-tuple-element.89), channel_id=1, source_target_pairs={{0,8},{8,0},{16,24},{24,16},{1,9},{9,1},{17,25},{25,17},{2,10},{10... | collective-permute-start | bytes 221192 | tf_op jit(solution)/shard_map/ppermute | solution.py:339
  436.3 26.2 %collective-permute-start.38 = (bf16[24,1536]{1,0:T(8,128)(2,1)S(1)}, bf16[24,1536]{1,0:T(8,128)(2,1)S(1)}, u32[]{:S(2)}, u32[]{:S(2)}) collective-permute-start(bf16[24,1536]{1,0:T(8,128)(2,1)S(1)} %get-tuple-element.91), channel_id=1, source_target_pairs={{0,16},{8,24},{16,0},{24,8},{1,17},{9,25},{17,1},{25,9},{2,18},{10... | collective-permute-start | bytes 221192 | tf_op jit(solution)/shard_map/ppermute | solution.py:339
  (90 other events, 784.3 us)
Sparse Core Ops, SparseCore 0:
  10.0 36.7 all-gather.2
  48.6 24.1 all-gather.4
where the time goes:
time: 508 us; the launch traced here: 499 us
  starting transfers between devices  179 us (35%)
  matrix products  102 us (20%)
  waiting for transfers between devices  90.2 us (18%)
  Pallas kernels  55.3 us (11%)
  other arithmetic  32.1 us (6%)
  local copies, waits for them, and re-layouts  23.9 us (5%)
  between operations  15.9 us (3%)
    ppermute x41, starting transfers between devices, swap(): return lax.ppermute(rows, axis, pairs)  91.4 us
    all_to_all x4, starting transfers between devices, exchange(): lax.all_to_all(row_data.reshape(shards, -1, model_width), 'exp', split_ax...  75.7 us
    ppermute x41, waiting for transfers between devices, swap(): return lax.ppermute(rows, axis, pairs)  61.1 us
    dot_general x13, matrix products, contract_last(): lax.dot_general(left, right, (((1,), (1,)), ((), ())), preferred_element_...  30.1 us
    dot_general x13, matrix products, contract_rows(): lax.dot_general(left, right, (((0,), (0,)), ((), ())), preferred_element_...  29.1 us
    pallas_call x1, Pallas kernels, attend_backward(): pl.pallas_call(functools.partial(backward_kernel, chunk=chunk), grid_spec...  27.3 us
    pallas_call x1, Pallas kernels, attend_forward(): pl.pallas_call(functools.partial(forward_kernel, chunk=chunk), grid_spec=...  20.7 us
    all_to_all x4, waiting for transfers between devices, exchange(): lax.all_to_all(row_data.reshape(shards, -1, model_width), 'exp', split_ax...  19.1 us
  transfers between devices with their start and end apart: 59, of which 19 were waited for; matrix products, arithmetic and copies ran while one was open for 26% of the time, Pallas kernels for 11%

commit v1 on v0

--- a/solution.py
+++ b/solution.py
@@ -309,6 +309,9 @@
             )
             for turn in range(2)
         ]
+        return got
+
+    def place_blocks(self, got):
         even = self.ctx % 2 == 0
         return jnp.stack([jnp.where(even, got[0], got[1]), jnp.where(even, got[1], got[0])])
 
@@ -353,25 +356,30 @@
             distance *= 2
         return held
 
-    def reduce_dense(self, part):
+    def sum_cores(self, part):
         rows = part.shape[0] // self.exp_count
-        pair_count = self.exp_count // 2
-        blocks = part.reshape(pair_count, 2, rows, part.shape[1])
+        blocks = part.reshape(self.exp_count // 2, 2, rows, part.shape[1])
         sent = lax.dynamic_index_in_dim(blocks, 1 - self.core, 1, keepdims=False)
         kept = lax.dynamic_index_in_dim(blocks, self.core, 1, keepdims=False)
-        both = add_low([kept, self.swap(sent, 1, "exp")])
+        return add_low([kept, self.swap(sent, 1, "exp")])
+
+    def sum_chips(self, blocks):
         pair = lax.axis_index("exp") // 2
-        parts = [lax.dynamic_index_in_dim(both, pair, 0, keepdims=False)]
-        for step in range(1, pair_count):
-            block = lax.dynamic_index_in_dim(both, pair ^ step, 0, keepdims=False)
+        parts = [lax.dynamic_index_in_dim(blocks, pair, 0, keepdims=False)]
+        for step in range(1, self.exp_count // 2):
+            block = lax.dynamic_index_in_dim(blocks, pair ^ step, 0, keepdims=False)
             parts.append(self.swap(block, 2 * step, "exp"))
-        total = add_low(parts)
-        cuts = total.reshape(self.ctx_count, rows // self.ctx_count, part.shape[1])
+        return add_low(parts)
+
+    def sum_ctx(self, total):
+        cuts = total.reshape(self.ctx_count, total.shape[0] // self.ctx_count, total.shape[1])
         parts = [lax.dynamic_index_in_dim(cuts, self.ctx, 0, keepdims=False)]
         for step in range(1, self.ctx_count):
             block = lax.dynamic_index_in_dim(cuts, self.ctx ^ step, 0, keepdims=False)
             parts.append(self.swap(block, step))
-        own = add_low(parts)
+        return add_low(parts)
+
+    def spread_ctx(self, own):
         every = jnp.stack([own] + [self.swap(own, step) for step in range(1, self.ctx_count)])
         return jnp.concatenate(
             [
@@ -442,8 +450,9 @@
     kept = codes % 2
 
     distances = list(range(2, layout.ctx_count, 2))
-    up_moved = [layout.swap(expert_up[0], step) for step in distances]
-    down_moved = [layout.swap(expert_down[0], step) for step in distances]
+    held_up, held_down = lax.optimization_barrier((expert_up[0], expert_down[0], grad_out_low))[:2]
+    up_moved = [layout.swap(held_up, step) for step in distances]
+    down_moved = [layout.swap(held_down, step) for step in distances]
 
     offset_count = buckets.shape[0]
     bucket_hot = buckets[None, :] == jnp.arange(bucket_count, dtype=jnp.int32)[:, None]
@@ -492,29 +501,28 @@
     def from_experts(summed):
         return jnp.dot(slot_hot, exchange(summed), preferred_element_type=jnp.float32)
 
-    grad_own = to_experts(grad_out_low)
-    grad_other = layout.swap(grad_own, 1)
-
     every_float = every_token.astype(jnp.float32)
     tokens_f = every_float[:token_count]
     normed_one, every_inverse = rms_forward(every_float, gain_first)
     inverse_one = every_inverse[:token_count]
-    hidden_one = after(normed_one.astype(jnp.bfloat16), grad_out_low)
+    hidden_one = normed_one.astype(jnp.bfloat16)
     queries = jnp.dot(
         hidden_one[:token_count], weight_joint[:, :model_width], preferred_element_type=jnp.float32
     ).astype(jnp.bfloat16) * jnp.bfloat16(SCORE_SCALE)
     key_values = jnp.dot(
         hidden_one, weight_joint[:, model_width:], preferred_element_type=jnp.float32
     ).astype(jnp.bfloat16)
+    grad_own = to_experts(after(grad_out_low, key_values))
+    grad_other = layout.swap(grad_own, 1)
     bases = layout.bases(token_count)
     attended, logsum = attend_forward(bases, queries, key_values, skew)
-    attended = after(attended, grad_own)
+    attended = after(attended, grad_own, *up_moved)
     attended_low = attended.astype(jnp.bfloat16)
     residual = tokens_f + jnp.dot(attended_low, weight_out, preferred_element_type=jnp.float32)
     normed_two, inverse_two = rms_forward(residual, gain_second)
     hidden_two = normed_two.astype(jnp.bfloat16)
 
-    row_own = after(to_experts(hidden_two), grad_other, *up_moved, *down_moved)
+    row_own = after(to_experts(hidden_two), grad_other, *down_moved)
     row_other = layout.swap(row_own, 1)
     ups = [expert_up[0]] + up_moved
     downs = [expert_down[0]] + down_moved
@@ -556,8 +564,7 @@
     grad_summed = sum_halves(grad_inputs[0], grad_inputs[1].astype(jnp.bfloat16))
     grad_back = from_experts(grad_summed)
     result_other = after(results[1].astype(jnp.bfloat16), grad_summed)
-    layer_rows = residual + from_experts(sum_halves(results[0], result_other))
-    layer_out = layout.return_blocks(layer_rows.astype(jnp.bfloat16))
+    result_summed = sum_halves(results[0], result_other)
 
     down_low = [part.astype(jnp.bfloat16) for part in grad_downs[1:]]
     up_low = [part.astype(jnp.bfloat16) for part in grad_ups[1:]]
@@ -579,12 +586,22 @@
     grad_mixed = grad_residual.astype(jnp.bfloat16)
     grad_weight_out = contract_rows(attended_low, grad_mixed)
     grad_attended = contract_last(grad_mixed, weight_out).astype(jnp.bfloat16)
-    out_sum = layout.reduce_dense(grad_weight_out.astype(jnp.bfloat16))
     grad_q, grad_k, grad_v, grad_off = attend_backward(
         bases, queries, grad_attended, attended, key_values, skew, logsum
     )
-    grad_k, *grads_down_moved = lax.optimization_barrier((grad_k, *grads_down_moved))
+    grad_k, result_summed = lax.optimization_barrier((grad_k, result_summed))
+    layer_rows = residual + from_experts(result_summed)
+    layer_sent = layout.return_blocks(layer_rows.astype(jnp.bfloat16))
+
     grad_kv = jnp.concatenate([grad_k, grad_v], axis=1)
+    kv_out_part = jnp.concatenate(
+        [
+            contract_rows(hidden_one, grad_kv).astype(jnp.bfloat16),
+            grad_weight_out.astype(jnp.bfloat16),
+        ],
+        axis=1,
+    )
+    kv_out_cores = layout.sum_cores(kv_out_part)
     partial_one = contract_last(grad_kv, weight_joint[:, model_width:])
     partial_own = contract_last(grad_q, weight_joint[:, :model_width])
     every_normed = every_float * every_inverse
@@ -592,15 +609,14 @@
         partial_own * every_normed[:token_count], axis=0
     )
     grad_hidden_one = layout.sum_rows(partial_one) + partial_own
+    grad_hidden_one, *grads_down_moved = lax.optimization_barrier(
+        (grad_hidden_one, *grads_down_moved)
+    )
+    grad_expert_down = own_slice(grad_downs[0], grads_down_moved)
+    kv_out_chips = layout.sum_chips(after(kv_out_cores, layer_rows, grad_hidden_one))
     grad_input_norm, _ = rms_backward(tokens_f, inverse_one, gain_first, grad_hidden_one)
-    grad_tokens = layout.return_blocks((grad_input_norm + grad_residual).astype(jnp.bfloat16)).astype(
-        jnp.float32
-    )
-    kv_sum = layout.reduce_dense(contract_rows(hidden_one, grad_kv).astype(jnp.bfloat16))
+    tokens_sent = layout.return_blocks((grad_input_norm + grad_residual).astype(jnp.bfloat16))
     query_part = contract_rows(hidden_one[:token_count], grad_q).astype(jnp.bfloat16)
-    query_part, *grads_up_moved = lax.optimization_barrier((query_part, *grads_up_moved))
-    grad_expert_up = own_slice(grad_ups[0], grads_up_moved)
-    grad_expert_down = own_slice(grad_downs[0], grads_down_moved)
     grad_table = jnp.dot(
         bucket_hot.astype(jnp.float32),
         grad_off.reshape(head_count, -1)[:, :offset_count].T,
@@ -612,7 +628,24 @@
     small_grads = jnp.concatenate([part.reshape(shards, -1) for part in small_grads], axis=1)
     small_grads = jnp.pad(small_grads, ((0, 0), (0, shard_rows * side_width - small_count)))
     side = small_grads.reshape(shards * shard_rows, side_width).astype(jnp.bfloat16)
-    query_sum = layout.reduce_dense(jnp.concatenate([query_part, side], axis=1))
+    query_cores = layout.sum_cores(jnp.concatenate([query_part, side], axis=1))
+    kv_out_chips, query_cores, *grads_up_moved = lax.optimization_barrier(
+        (kv_out_chips, query_cores, *grads_up_moved)
+    )
+    grad_expert_up = own_slice(grad_ups[0], grads_up_moved)
+    kv_out_own = layout.sum_ctx(kv_out_chips)
+    query_chips = layout.sum_chips(query_cores)
+    kv_out_own, query_chips = lax.optimization_barrier((kv_out_own, query_chips))
+    kv_out_sum = layout.spread_ctx(kv_out_own)
+    query_own = layout.sum_ctx(query_chips)
+    kv_out_sum, query_own = lax.optimization_barrier((kv_out_sum, query_own))
+    query_sum = layout.spread_ctx(query_own)
+    layer_out = layout.place_blocks([after(part, kv_out_own) for part in layer_sent])
+    grad_tokens = layout.place_blocks([after(part, kv_out_sum) for part in tokens_sent]).astype(
+        jnp.float32
+    )
+    kv_sum = kv_out_sum[:, : 2 * model_width]
+    out_sum = kv_out_sum[:, 2 * model_width :]
     side_sum = query_sum[:, model_width:].reshape(-1)[:small_count].astype(jnp.float32)
     joint_sum = jnp.concatenate([query_sum[:, :model_width], kv_sum], axis=1)
     sum_gain_one, sum_gain_two, sum_router, sum_table = jnp.split(side_sum, small_cuts)

time: 508 us -> 496 us (0.976)
  starting transfers between devices: 179 us -> 93.9 us
  waiting for transfers between devices: 90.2 us -> 157 us
    ppermute x41 -> x31, waiting for transfers between devices: 61.1 us -> 149 us  [swap(): return lax.ppermute(rows, axis, pairs)]
    all_to_all x4, starting transfers between devices: 75.7 us -> 15.5 us  [exchange(): lax.all_to_all(row_data.reshape(shards, -1, model_width), 'exp', split_ax...]
    ppermute x41 -> x31, starting transfers between devices: 91.4 us -> 54.4 us  [swap(): return lax.ppermute(rows, axis, pairs)]
    ppermute x1, starting transfers between devices: 0.07 us -> 15.2 us  [all_rows(): lax.ppermute(rows, BOTH, self.member_pairs(shift))]
    all_to_all x4, waiting for transfers between devices: 19.1 us -> 5.06 us  [exchange(): lax.all_to_all(row_data.reshape(shards, -1, model_width), 'exp', split_ax...]
    ppermute x4, waiting for transfers between devices: 7.21 us -> 0.01 us  [return_blocks(): lax.ppermute(lax.dynamic_index_in_dim(blocks, (turn + self.side) % 2, 0,...]
    unnamed x113 -> x131, local copies, waits for them, and re-layouts: 13.3 us -> 13.4 us
  transfers between devices with their start and end apart: 59 -> 49, of which waited for: 19 -> 17; matrix products, arithmetic and copies ran while one was open for 26% -> 28% of each run, Pallas kernels for 11% -> 11%
where the time goes in v1:
time: 496 us; the launch traced here: 486 us
  waiting for transfers between devices  157 us (32%)
  matrix products  106 us (21%)
  starting transfers between devices  93.9 us (19%)
  Pallas kernels  55.3 us (11%)
  other arithmetic  32.4 us (7%)
  local copies, waits for them, and re-layouts  26 us (5%)
  between operations  15.7 us (3%)
    ppermute x31, waiting for transfers between devices, swap(): return lax.ppermute(rows, axis, pairs)  149 us
    ppermute x31, starting transfers between devices, swap(): return lax.ppermute(rows, axis, pairs)  54.4 us
    dot_general x13, matrix products, contract_rows(): lax.dot_general(left, right, (((0,), (0,)), ((), ())), preferred_element_...  32.4 us
    dot_general x13, matrix products, contract_last(): lax.dot_general(left, right, (((1,), (1,)), ((), ())), preferred_element_...  29.3 us
    pallas_call x1, Pallas kernels, attend_backward(): pl.pallas_call(functools.partial(backward_kernel, chunk=chunk), grid_spec...  27.3 us
    pallas_call x1, Pallas kernels, attend_forward(): pl.pallas_call(functools.partial(forward_kernel, chunk=chunk), grid_spec=...  20.7 us
    all_to_all x4, starting transfers between devices, exchange(): lax.all_to_all(row_data.reshape(shards, -1, model_width), 'exp', split_ax...  15.5 us
    ppermute x1, starting transfers between devices, all_rows(): lax.ppermute(rows, BOTH, self.member_pairs(shift))  15.2 us
  transfers between devices with their start and end apart: 49, of which 17 were waited for; matrix products, arithmetic and copies ran while one was open for 28% of the time, Pallas kernels for 11%

profile of v1, /device:TPU:0, one launch (start us, length us, event | category | flops | bytes accessed | tf_op | source)
XLA Modules:
  0.0 486.4 jit_solution(18398858483901586426)
XLA Ops:
  30.0 15.2 %collective-permute-start.2 = (bf16[512,768]{1,0:T(8,128)(2,1)S(1)}, bf16[512,768]{1,0:T(8,128)(2,1)S(1)}, u32[]{:S(2)}, u32[]{:S(2)}) collective-permute-start(bf16[512,768]{1,0:T(8,128)(2,1)S(1)} %pad_maximum_fusion.2), channel_id=1, source_target_pairs={{0,1},{1,0},{2,3},{3,2},{4,5},{5,4},{6,7},{7,6},{8,9},{9,8},{10,11... | collective-permute-start | bytes 2359304 | tf_op jit(solution)/shard_map/ppermute | solution.py:321
  48.7 10.1 %collective-permute-start.10 = (bf16[768,768]{1,0:T(8,128)(2,1)}, bf16[768,768]{1,0:T(8,128)(2,1)}, u32[]{:S(2)}, u32[]{:S(2)}) collective-permute-start(bf16[768,768]{1,0:T(8,128)(2,1)} %bitcast.11), channel_id=1, source_target_pairs={{0,16},{8,24},{16,0},{24,8},{1,17},{9,25},{17,1},{25,9},{2,18},{10... | collective-permute-start | bytes 3538952 | tf_op jit(solution)/shard_map/ppermute | solution.py:342
  61.2 6.2 %convolution_convert_fusion.k_ref.v_ref = bf16[1024,1536]{1,0:T(8,128)(2,1)} fusion(bf16[1024,768]{1,0:T(8,128)(2,1)S(1)} %get-tuple-element.86, bf16[768,2304]{1,0:T(8,128)(2,1)} %all-gather.3.cloned.1.call-done), kind=kOutput, calls=%fused_computation | convolution fusion | flops 2417491968 | bytes 7077888 | tf_op jit(solution)/shard_map/dot_general | solution.py:512
  73.6 7.4 %skew_bias.1.skew_ref = bf16[12,1920,128]{2,1,0:T(8,128)(2,1)} custom-call(f32[12,1,2048]{2,1,0:T(1,128)S(1)} %reshape.434.offset_ref), custom_call_target="tpu_custom_call" | custom-call | tf_op jit(solution)/shard_map/skew_bias/pallas_call | solution.py:43
  85.3 20.7 %attend_forward.1 = (f32[512,768]{1,0:T(8,128)S(1)}, f32[6,2,512]{2,1,0:T(2,128)S(1)}) custom-call(s32[2]{0:T(128)S(1)} %pad_add_fusion.1.base_ref, bf16[512,768]{1,0:T(8,128)(2,1)S(1)} %fusion.45.q_ref, bf16[1024,1536]{1,0:T(8,128)(2,1)} %convolution_convert_fusion.k_ref.v_ref, bf16[1024,1536]{1,0:T(8,128)(2,1)} %convolution_convert_fusion.k_ref.v_ref, ...), custom_call_target="tpu_custom_call" | custom-call | tf_op jit(solution)/shard_map/attend_forward/pallas_call | solution.py:107
  108.8 24.5 %collective-permute-done.10 = bf16[768,768]{1,0:T(8,128)(2,1)} collective-permute-done((bf16[768,768]{1,0:T(8,128)(2,1)}, bf16[768,768]{1,0:T(8,128)(2,1)}, u32[]{:S(2)}, u32[]{:S(2)}) %collective-permute-start.10) | collective-permute-done | bytes 1179680 | tf_op jit(solution)/shard_map/ppermute | solution.py:342
  143.4 15.0 %collective-permute-done.12 = bf16[768,768]{1,0:T(8,128)(2,1)} collective-permute-done((bf16[768,768]{1,0:T(8,128)(2,1)}, bf16[768,768]{1,0:T(8,128)(2,1)}, u32[]{:S(2)}, u32[]{:S(2)}) %collective-permute-start.12) | collective-permute-done | bytes 1179680 | tf_op jit(solution)/shard_map/ppermute | solution.py:342
  158.4 20.2 %collective-permute-done.11 = bf16[640,768]{1,0:T(8,128)(2,1)} collective-permute-done((bf16[640,768]{1,0:T(8,128)(2,1)S(1)}, bf16[640,768]{1,0:T(8,128)(2,1)}, u32[]{:S(2)}, u32[]{:S(2)}) %collective-permute-start.11) | collective-permute-done | bytes 983072 | tf_op jit(solution)/shard_map/ppermute | solution.py:342
  181.3 4.2 fusion.154
  188.1 13.9 %collective-permute-done.13 = bf16[640,768]{1,0:T(8,128)(2,1)S(1)} collective-permute-done((bf16[640,768]{1,0:T(8,128)(2,1)S(1)}, bf16[640,768]{1,0:T(8,128)(2,1)S(1)}, u32[]{:S(2)}, u32[]{:S(2)}) %collective-permute-start.13) | collective-permute-done | bytes 983072 | tf_op jit(solution)/shard_map/ppermute | solution.py:342
  203.7 5.3 %fusion.4 = (bf16[640,768]{1,0:T(8,128)(2,1)S(1)}, f32[640]{0:T(1024)S(1)}, f32[640,768]{1,0:T(8,128)}) fusion(f32[640]{0:T(1024)S(1)} %get-tuple-element.78, bf16[8,80,768]{2,1,0:T(8,128)(2,1)S(1)} %all-to-all-done, f32[640,768]{1,0:T(8,128)} %fusion.125, bf16[768,768]{1,0:T(8,128)(2,1)} %collective-permute-done.12, f32[640,768]{1,0:T(8,128)} %fusion.154), kind=kOutput, calls=%fused_computation.27 | convolution fusion | flops 762346880 | bytes 9049088 | tf_op jit(solution)/shard_map/dot_general | solution.py:552
  224.4 4.0 multiply_convert_fusion.1
  257.4 26.7 %collective-permute-done.14 = bf16[640,768]{1,0:T(8,128)(2,1)S(1)} collective-permute-done((bf16[640,768]{1,0:T(8,128)(2,1)S(1)}, bf16[640,768]{1,0:T(8,128)(2,1)S(1)}, u32[]{:S(2)}, u32[]{:S(2)}) %collective-permute-start.14) | collective-permute-done | bytes 983072 | tf_op jit(solution)/shard_map/ppermute | solution.py:342
  291.7 4.7 fusion.141
  296.4 4.3 fusion.143
  300.7 5.0 %all-to-all-done.2 = bf16[8,80,768]{2,1,0:T(8,128)(2,1)S(1)} async-done(((bf16[8,80,768]{2,1,0:T(8,128)(2,1)}), bf16[8,80,768]{2,1,0:T(8,128)(2,1)S(1)}, u32[]{:S(2)}, u32[]{:S(2)}) %all-to-all-start.2) | async-done | bytes 983072 | tf_op jit(solution)/shard_map/all_to_all | solution.py:487
  308.9 27.3 %attend_backward.1 = (bf16[512,768]{1,0:T(8,128)(2,1)S(1)}, bf16[1024,768]{1,0:T(8,128)(2,1)S(1)}, bf16[1024,768]{1,0:T(8,128)(2,1)}, f32[6,2,2048]{2,1,0:T(2,128)S(1)}) custom-call(s32[2]{0:T(128)S(1)} %pad_add_fusion.1.base_ref, bf16[512,768]{1,0:T(8,128)(2,1)S(1)} %fusion.45.q_ref, bf16[512,768]{1,0:T(8,128)(2,1)S(1)} %convolution_convert_fusion.6.do_ref, ...), custom_call_target="tpu_custom_call" | custom-call | tf_op jit(solution)/shard_map/attend_backward/pallas_call | solution.py:205
  347.5 4.2 convolution_convert_fusion.1
  356.9 4.2 all-to-all-start.3
  395.4 7.4 %collective-permute-done.20 = bf16[96,2304]{1,0:T(8,128)(2,1)S(1)} collective-permute-done((bf16[96,2304]{1,0:T(8,128)(2,1)S(1)}, bf16[96,2304]{1,0:T(8,128)(2,1)S(1)}, u32[]{:S(2)}, u32[]{:S(2)}) %collective-permute-start.20) | collective-permute-done | bytes 442400 | tf_op jit(solution)/shard_map/ppermute | solution.py:342
  402.9 10.2 %collective-permute-done.21 = bf16[96,2304]{1,0:T(8,128)(2,1)S(1)} collective-permute-done((bf16[96,2304]{1,0:T(8,128)(2,1)S(1)}, bf16[96,2304]{1,0:T(8,128)(2,1)S(1)}, u32[]{:S(2)}, u32[]{:S(2)}) %collective-permute-start.21) | collective-permute-done | bytes 442400 | tf_op jit(solution)/shard_map/ppermute | solution.py:342
  442.8 4.1 collective-permute-start.34
  448.3 7.2 %collective-permute-done.33 = bf16[24,2304]{1,0:T(8,128)(2,1)S(1)} collective-permute-done((bf16[24,2304]{1,0:T(8,128)(2,1)S(1)}, bf16[24,2304]{1,0:T(8,128)(2,1)S(1)}, u32[]{:S(2)}, u32[]{:S(2)}) %collective-permute-start.33) | collective-permute-done | bytes 110624 | tf_op jit(solution)/shard_map/ppermute | solution.py:342
  455.5 11.3 %collective-permute-done.34 = bf16[24,2304]{1,0:T(8,128)(2,1)S(1)} collective-permute-done((bf16[24,2304]{1,0:T(8,128)(2,1)S(1)}, bf16[24,2304]{1,0:T(8,128)(2,1)S(1)}, u32[]{:S(2)}, u32[]{:S(2)}) %collective-permute-start.34) | collective-permute-done | bytes 110624 | tf_op jit(solution)/shard_map/ppermute | solution.py:342
  (355 shorter events, 207.4 us)
Async XLA Ops:
  7.2 54.0 %all-gather.3.cloned.1.call-start = ((), (), s32[]{:S(2)}) async-start(), calls=%async_computation.4 | async-start | bytes 3981312 | tf_op jit(solution)/shard_map/all_gather | solution.py:442
  8.0 125.3 %all-gather.5.cloned.1.call-start = ((), (), s32[]{:S(2)}) async-start(), calls=%async_computation.5 | async-start | bytes 1327104 | tf_op jit(solution)/shard_map/all_gather | solution.py:443
  9.2 20.7 %collective-permute-start = (bf16[256,768]{1,0:T(8,128)(2,1)S(1)}, bf16[256,768]{1,0:T(8,128)(2,1)S(1)}, u32[]{:S(2)}, u32[]{:S(2)}) collective-permute-start(bf16[256,768]{1,0:T(8,128)(2,1)S(1)} %get-tuple-element.105), channel_id=1, source_target_pairs={{0,0},{1,16},{2,2},{3,18},{4,4},{5,20},{6,6},{7,22},{8,8},{9,24},{... | collective-permute-start | bytes 1179656 | tf_op jit(solution)/shard_map/ppermute | solution.py:291
  19.0 27.6 %collective-permute-start.8 = (bf16[256,768]{1,0:T(8,128)(2,1)S(1)}, bf16[256,768]{1,0:T(8,128)(2,1)S(1)}, u32[]{:S(2)}, u32[]{:S(2)}) collective-permute-start(bf16[256,768]{1,0:T(8,128)(2,1)S(1)} %get-tuple-element.101), channel_id=1, source_target_pairs={{0,0},{1,16},{2,2},{3,18},{4,4},{5,20},{6,6},{7,22},{8,8},{9,24},{... | collective-permute-start | bytes 1179656 | tf_op jit(solution)/shard_map/ppermute | solution.py:291
  21.9 24.6 %collective-permute-start.9 = (bf16[256,768]{1,0:T(8,128)(2,1)S(1)}, bf16[256,768]{1,0:T(8,128)(2,1)}, u32[]{:S(2)}, u32[]{:S(2)}) collective-permute-start(bf16[256,768]{1,0:T(8,128)(2,1)S(1)} %get-tuple-element.102), channel_id=1, source_target_pairs={{0,8},{1,24},{2,10},{3,26},{4,12},{5,28},{6,14},{7,30},{8,0},{9,16... | collective-permute-start | bytes 1179656 | tf_op jit(solution)/shard_map/ppermute | solution.py:291
  30.0 28.7 %collective-permute-start.2 = (bf16[512,768]{1,0:T(8,128)(2,1)S(1)}, bf16[512,768]{1,0:T(8,128)(2,1)S(1)}, u32[]{:S(2)}, u32[]{:S(2)}) collective-permute-start(bf16[512,768]{1,0:T(8,128)(2,1)S(1)} %pad_maximum_fusion.2), channel_id=1, source_target_pairs={{0,1},{1,0},{2,3},{3,2},{4,5},{5,4},{6,7},{7,6},{8,9},{9,8},{10,11... | collective-permute-start | bytes 2359304 | tf_op jit(solution)/shard_map/ppermute | solution.py:321
  48.7 84.5 %collective-permute-start.10 = (bf16[768,768]{1,0:T(8,128)(2,1)}, bf16[768,768]{1,0:T(8,128)(2,1)}, u32[]{:S(2)}, u32[]{:S(2)}) collective-permute-start(bf16[768,768]{1,0:T(8,128)(2,1)} %bitcast.11), channel_id=1, source_target_pairs={{0,16},{8,24},{16,0},{24,8},{1,17},{9,25},{17,1},{25,9},{2,18},{10... | collective-permute-start | bytes 3538952 | tf_op jit(solution)/shard_map/ppermute | solution.py:342
  69.3 36.7 %all-to-all-start = ((bf16[8,80,768]{2,1,0:T(8,128)(2,1)}), bf16[8,80,768]{2,1,0:T(8,128)(2,1)S(1)}, u32[]{:S(2)}, u32[]{:S(2)}) async-start(bf16[8,80,768]{2,1,0:T(8,128)(2,1)} %bitcast.213), calls=%async_computation | async-start | bytes 1966080 | tf_op jit(solution)/shard_map/all_to_all | solution.py:487
  81.0 77.4 %collective-permute-start.12 = (bf16[768,768]{1,0:T(8,128)(2,1)}, bf16[768,768]{1,0:T(8,128)(2,1)}, u32[]{:S(2)}, u32[]{:S(2)}) collective-permute-start(bf16[768,768]{1,0:T(8,128)(2,1)} %bitcast.230), channel_id=1, source_target_pairs={{0,16},{8,24},{16,0},{24,8},{1,17},{9,25},{17,1},{25,9},{2,18},{10... | collective-permute-start | bytes 3538952 | tf_op jit(solution)/shard_map/ppermute | solution.py:342
  106.0 72.7 %collective-permute-start.11 = (bf16[640,768]{1,0:T(8,128)(2,1)S(1)}, bf16[640,768]{1,0:T(8,128)(2,1)}, u32[]{:S(2)}, u32[]{:S(2)}) collective-permute-start(bf16[640,768]{1,0:T(8,128)(2,1)S(1)} %bitcast.207), channel_id=1, source_target_pairs={{0,8},{8,0},{16,24},{24,16},{1,9},{9,1},{17,25},{25,17},{2,10},{10... | collective-permute-start | bytes 2949128 | tf_op jit(solution)/shard_map/ppermute | solution.py:342
  178.7 23.4 %collective-permute-start.13 = (bf16[640,768]{1,0:T(8,128)(2,1)S(1)}, bf16[640,768]{1,0:T(8,128)(2,1)S(1)}, u32[]{:S(2)}, u32[]{:S(2)}) collective-permute-start(bf16[640,768]{1,0:T(8,128)(2,1)S(1)} %bitcast.198), channel_id=1, source_target_pairs={{0,8},{8,0},{16,24},{24,16},{1,9},{9,1},{17,25},{25,17},{2,10},{10... | collective-permute-start | bytes 2949128 | tf_op jit(solution)/shard_map/ppermute | solution.py:342
  216.6 155.6 %collective-permute-start.19 = (bf16[768,768]{1,0:T(8,128)(2,1)}, bf16[768,768]{1,0:T(8,128)(2,1)}, u32[]{:S(2)}, u32[]{:S(2)}) collective-permute-start(bf16[768,768]{1,0:T(8,128)(2,1)} %add_convert_fusion.1), channel_id=1, source_target_pairs={{0,16},{8,24},{16,0},{24,8},{1,17},{9,25},{17,1},{25,9},{2,18},{10... | collective-permute-start | bytes 3538952 | tf_op jit(solution)/shard_map/ppermute | solution.py:342
  240.4 43.7 %collective-permute-start.14 = (bf16[640,768]{1,0:T(8,128)(2,1)S(1)}, bf16[640,768]{1,0:T(8,128)(2,1)S(1)}, u32[]{:S(2)}, u32[]{:S(2)}) collective-permute-start(bf16[640,768]{1,0:T(8,128)(2,1)S(1)} %add_convert_fusion.4), channel_id=1, source_target_pairs={{0,8},{8,0},{16,24},{24,16},{1,9},{9,1},{17,25},{25,17},{2,10},{10... | collective-permute-start | bytes 2949128 | tf_op jit(solution)/shard_map/ppermute | solution.py:342
  248.7 164.6 %collective-permute-start.24 = (bf16[768,768]{1,0:T(8,128)(2,1)}, bf16[768,768]{1,0:T(8,128)(2,1)}, u32[]{:S(2)}, u32[]{:S(2)}) collective-permute-start(bf16[768,768]{1,0:T(8,128)(2,1)} %add_convert_fusion), channel_id=1, source_target_pairs={{0,16},{8,24},{16,0},{24,8},{1,17},{9,25},{17,1},{25,9},{2,18},{10... | collective-permute-start | bytes 3538952 | tf_op jit(solution)/shard_map/ppermute | solution.py:342
  300.7 42.3 %collective-permute-start.15 = (bf16[640,768]{1,0:T(8,128)(2,1)}, bf16[640,768]{1,0:T(8,128)(2,1)}, u32[]{:S(2)}, u32[]{:S(2)}) collective-permute-start(bf16[640,768]{1,0:T(8,128)(2,1)} %get-tuple-element.46), channel_id=1, source_target_pairs={{0,8},{8,0},{16,24},{24,16},{1,9},{9,1},{17,25},{25,17},{2,10},{10... | collective-permute-start | bytes 2949128 | tf_op jit(solution)/shard_map/ppermute | solution.py:342
  356.9 28.1 %all-to-all-start.3 = ((bf16[8,80,768]{2,1,0:T(8,128)(2,1)}), bf16[8,80,768]{2,1,0:T(8,128)(2,1)}, u32[]{:S(2)}, u32[]{:S(2)}) async-start(bf16[8,80,768]{2,1,0:T(8,128)(2,1)} %bitcast.208), calls=%async_computation.3 | async-start | bytes 1966080 | tf_op jit(solution)/shard_map/all_to_all | solution.py:487
  364.6 23.1 %collective-permute-start.17 = (bf16[4,96,2304]{2,1,0:T(8,128)(2,1)}, bf16[4,96,2304]{2,1,0:T(8,128)(2,1)}, u32[]{:S(2)}, u32[]{:S(2)}) collective-permute-start(bf16[4,96,2304]{2,1,0:T(8,128)(2,1)} %dynamic-slice_bitcast_fusion), channel_id=1, source_target_pairs={{0,1},{1,0},{2,3},{3,2},{4,5},{5,4},{6,7},{7,6},{8,9},{9,8},{10,11... | collective-permute-start | bytes 5308424 | tf_op jit(solution)/shard_map/ppermute | solution.py:342
  391.4 21.6 %collective-permute-start.21 = (bf16[96,2304]{1,0:T(8,128)(2,1)S(1)}, bf16[96,2304]{1,0:T(8,128)(2,1)S(1)}, u32[]{:S(2)}, u32[]{:S(2)}) collective-permute-start(bf16[96,2304]{1,0:T(8,128)(2,1)S(1)} %get-tuple-element.84), channel_id=1, source_target_pairs={{0,4},{1,5},{2,6},{3,7},{4,0},{5,1},{6,2},{7,3},{8,12},{9,13},{10,... | collective-permute-start | bytes 1327112 | tf_op jit(solution)/shard_map/ppermute | solution.py:342
  392.9 20.1 %collective-permute-start.22 = (bf16[96,2304]{1,0:T(8,128)(2,1)S(1)}, bf16[96,2304]{1,0:T(8,128)(2,1)S(1)}, u32[]{:S(2)}, u32[]{:S(2)}) collective-permute-start(bf16[96,2304]{1,0:T(8,128)(2,1)S(1)} %get-tuple-element.83), channel_id=1, source_target_pairs={{0,6},{1,7},{2,4},{3,5},{4,2},{5,3},{6,0},{7,1},{8,14},{9,15},{10,... | collective-permute-start | bytes 1327112 | tf_op jit(solution)/shard_map/ppermute | solution.py:342
  393.5 46.5 %collective-permute-start.16 = (bf16[256,768]{1,0:T(8,128)(2,1)S(1)}, bf16[256,768]{1,0:T(8,128)(2,1)S(1)}, u32[]{:S(2)}, u32[]{:S(2)}) collective-permute-start(bf16[256,768]{1,0:T(8,128)(2,1)S(1)} %get-tuple-element.97), channel_id=1, source_target_pairs={{0,0},{16,1},{2,2},{18,3},{4,4},{20,5},{6,6},{22,7},{8,8},{24,9},{... | collective-permute-start | bytes 1179656 | tf_op jit(solution)/shard_map/ppermute | solution.py:305
  402.8 37.1 %collective-permute-start.31 = (bf16[256,768]{1,0:T(8,128)(2,1)S(1)}, bf16[256,768]{1,0:T(8,128)(2,1)S(1)}, u32[]{:S(2)}, u32[]{:S(2)}) collective-permute-start(bf16[256,768]{1,0:T(8,128)(2,1)S(1)} %get-tuple-element.98), channel_id=1, source_target_pairs={{8,0},{24,1},{10,2},{26,3},{12,4},{28,5},{14,6},{30,7},{0,8},{16,9... | collective-permute-start | bytes 1179656 | tf_op jit(solution)/shard_map/ppermute | solution.py:305
  440.0 31.4 %collective-permute-start.39 = (bf16[256,768]{1,0:T(8,128)(2,1)S(1)}, bf16[256,768]{1,0:T(8,128)(2,1)S(1)}, u32[]{:S(2)}, u32[]{:S(2)}) collective-permute-start(bf16[256,768]{1,0:T(8,128)(2,1)S(1)} %get-tuple-element.94), channel_id=1, source_target_pairs={{8,0},{24,1},{10,2},{26,3},{12,4},{28,5},{14,6},{30,7},{0,8},{16,9... | collective-permute-start | bytes 1179656 | tf_op jit(solution)/shard_map/ppermute | solution.py:305
  440.0 32.2 %collective-permute-start.32 = (bf16[256,768]{1,0:T(8,128)(2,1)S(1)}, bf16[256,768]{1,0:T(8,128)(2,1)S(1)}, u32[]{:S(2)}, u32[]{:S(2)}) collective-permute-start(bf16[256,768]{1,0:T(8,128)(2,1)S(1)} %get-tuple-element.93), channel_id=1, source_target_pairs={{0,0},{16,1},{2,2},{18,3},{4,4},{20,5},{6,6},{22,7},{8,8},{24,9},{... | collective-permute-start | bytes 1179656 | tf_op jit(solution)/shard_map/ppermute | solution.py:305
  442.8 24.0 %collective-permute-start.34 = (bf16[24,2304]{1,0:T(8,128)(2,1)S(1)}, bf16[24,2304]{1,0:T(8,128)(2,1)S(1)}, u32[]{:S(2)}, u32[]{:S(2)}) collective-permute-start(bf16[24,2304]{1,0:T(8,128)(2,1)S(1)} %fusion.94), channel_id=1, source_target_pairs={{0,16},{8,24},{16,0},{24,8},{1,17},{9,25},{17,1},{25,9},{2,18},{10... | collective-permute-start | bytes 331784 | tf_op jit(solution)/shard_map/ppermute | solution.py:342
  (89 other events, 768.6 us)
Sparse Core Ops, SparseCore 0:
  10.0 37.6 all-gather.2
  49.6 23.2 all-gather.4

commit v2 on v1

--- a/solution.py
+++ b/solution.py
@@ -450,7 +450,8 @@
     kept = codes % 2
 
     distances = list(range(2, layout.ctx_count, 2))
-    held_up, held_down = lax.optimization_barrier((expert_up[0], expert_down[0], grad_out_low))[:2]
+    held_up = after(expert_up[0], tokens)
+    held_down = after(expert_down[0], grad_out_low)
     up_moved = [layout.swap(held_up, step) for step in distances]
     down_moved = [layout.swap(held_down, step) for step in distances]
 
@@ -566,8 +567,8 @@
     result_other = after(results[1].astype(jnp.bfloat16), grad_summed)
     result_summed = sum_halves(results[0], result_other)
 
-    down_low = [part.astype(jnp.bfloat16) for part in grad_downs[1:]]
-    up_low = [part.astype(jnp.bfloat16) for part in grad_ups[1:]]
+    down_low = [after(part.astype(jnp.bfloat16), grad_summed) for part in grad_downs[1:]]
+    up_low = [after(part.astype(jnp.bfloat16), grad_summed) for part in grad_ups[1:]]
 
     def moved(parts):
         return [layout.swap(part, step) for part, step in zip(parts, distances)]
@@ -602,18 +603,14 @@
         axis=1,
     )
     kv_out_cores = layout.sum_cores(kv_out_part)
-    partial_one = contract_last(grad_kv, weight_joint[:, model_width:])
+    partial_one = contract_last(after(grad_kv, kv_out_part), weight_joint[:, model_width:])
     partial_own = contract_last(grad_q, weight_joint[:, :model_width])
     every_normed = every_float * every_inverse
     grad_gain_one = jnp.sum(partial_one * every_normed, axis=0) + jnp.sum(
         partial_own * every_normed[:token_count], axis=0
     )
     grad_hidden_one = layout.sum_rows(partial_one) + partial_own
-    grad_hidden_one, *grads_down_moved = lax.optimization_barrier(
-        (grad_hidden_one, *grads_down_moved)
-    )
-    grad_expert_down = own_slice(grad_downs[0], grads_down_moved)
-    kv_out_chips = layout.sum_chips(after(kv_out_cores, layer_rows, grad_hidden_one))
+    kv_out_chips = layout.sum_chips(after(kv_out_cores, layer_rows, partial_own))
     grad_input_norm, _ = rms_backward(tokens_f, inverse_one, gain_first, grad_hidden_one)
     tokens_sent = layout.return_blocks((grad_input_norm + grad_residual).astype(jnp.bfloat16))
     query_part = contract_rows(hidden_one[:token_count], grad_q).astype(jnp.bfloat16)
@@ -629,16 +626,17 @@
     small_grads = jnp.pad(small_grads, ((0, 0), (0, shard_rows * side_width - small_count)))
     side = small_grads.reshape(shards * shard_rows, side_width).astype(jnp.bfloat16)
     query_cores = layout.sum_cores(jnp.concatenate([query_part, side], axis=1))
-    kv_out_chips, query_cores, *grads_up_moved = lax.optimization_barrier(
-        (kv_out_chips, query_cores, *grads_up_moved)
-    )
-    grad_expert_up = own_slice(grad_ups[0], grads_up_moved)
+    kv_out_chips, query_cores, grads_down_moved, grads_up_moved = lax.optimization_barrier(
+        (kv_out_chips, query_cores, grads_down_moved, grads_up_moved)
+    )
+    grad_expert_down = own_slice(grad_downs[0], grads_down_moved)
     kv_out_own = layout.sum_ctx(kv_out_chips)
     query_chips = layout.sum_chips(query_cores)
     kv_out_own, query_chips = lax.optimization_barrier((kv_out_own, query_chips))
     kv_out_sum = layout.spread_ctx(kv_out_own)
     query_own = layout.sum_ctx(query_chips)
     kv_out_sum, query_own = lax.optimization_barrier((kv_out_sum, query_own))
+    grad_expert_up = own_slice(grad_ups[0], grads_up_moved)
     query_sum = layout.spread_ctx(query_own)
     layer_out = layout.place_blocks([after(part, kv_out_own) for part in layer_sent])
     grad_tokens = layout.place_blocks([after(part, kv_out_sum) for part in tokens_sent]).astype(

time: 496 us -> 497 us (level)
  waiting for transfers between devices: 157 us -> 125 us
  starting transfers between devices: 93.9 us -> 125 us
    all_to_all x4, starting transfers between devices: 15.5 us -> 44.4 us  [exchange(): lax.all_to_all(row_data.reshape(shards, -1, model_width), 'exp', split_ax...]
    ppermute x31, waiting for transfers between devices: 149 us -> 122 us  [swap(): return lax.ppermute(rows, axis, pairs)]
    all_to_all x4, waiting for transfers between devices: 5.06 us -> 0.01 us  [exchange(): lax.all_to_all(row_data.reshape(shards, -1, model_width), 'exp', split_ax...]
    unnamed x131 -> x139, local copies, waits for them, and re-layouts: 13.4 us -> 13.6 us
  transfers between devices with their start and end apart: 49 -> 49, of which waited for: 17 -> 15; matrix products, arithmetic and copies ran while one was open for 28% -> 23% of each run, Pallas kernels for 11% -> 11%
where the time goes in v2:
time: 497 us; the launch traced here: 488 us
  starting transfers between devices  125 us (25%)
  waiting for transfers between devices  125 us (25%)
  matrix products  108 us (22%)
  Pallas kernels  55.3 us (11%)
  other arithmetic  32 us (6%)
  local copies, waits for them, and re-layouts  27.6 us (6%)
  between operations  15.9 us (3%)
    ppermute x31, waiting for transfers between devices, swap(): return lax.ppermute(rows, axis, pairs)  122 us
    ppermute x31, starting transfers between devices, swap(): return lax.ppermute(rows, axis, pairs)  54.7 us
    all_to_all x4, starting transfers between devices, exchange(): lax.all_to_all(row_data.reshape(shards, -1, model_width), 'exp', split_ax...  44.4 us
    dot_general x13, matrix products, contract_last(): lax.dot_general(left, right, (((1,), (1,)), ((), ())), preferred_element_...  33 us
    dot_general x13, matrix products, contract_rows(): lax.dot_general(left, right, (((0,), (0,)), ((), ())), preferred_element_...  32.1 us
    pallas_call x1, Pallas kernels, attend_backward(): pl.pallas_call(functools.partial(backward_kernel, chunk=chunk), grid_spec...  27.3 us
    pallas_call x1, Pallas kernels, attend_forward(): pl.pallas_call(functools.partial(forward_kernel, chunk=chunk), grid_spec=...  20.7 us
    ppermute x1, starting transfers between devices, all_rows(): lax.ppermute(rows, BOTH, self.member_pairs(shift))  15.4 us
  transfers between devices with their start and end apart: 49, of which 15 were waited for; matrix products, arithmetic and copies ran while one was open for 23% of the time, Pallas kernels for 11%

profile of v2, /device:TPU:0, one launch (start us, length us, event | category | flops | bytes accessed | tf_op | source)
XLA Modules:
  0.0 488.3 jit_solution(14653581452055482676)
XLA Ops:
  29.9 15.4 %collective-permute-start.2 = (bf16[512,768]{1,0:T(8,128)(2,1)S(1)}, bf16[512,768]{1,0:T(8,128)(2,1)S(1)}, u32[]{:S(2)}, u32[]{:S(2)}) collective-permute-start(bf16[512,768]{1,0:T(8,128)(2,1)S(1)} %pad_maximum_fusion.2), channel_id=1, source_target_pairs={{0,1},{1,0},{2,3},{3,2},{4,5},{5,4},{6,7},{7,6},{8,9},{9,8},{10,11... | collective-permute-start | bytes 2359304 | tf_op jit(solution)/shard_map/ppermute | solution.py:321
  55.8 6.2 %convolution_convert_fusion.k_ref.v_ref = bf16[1024,1536]{1,0:T(8,128)(2,1)} fusion(bf16[1024,768]{1,0:T(8,128)(2,1)S(1)} %get-tuple-element.92, bf16[768,2304]{1,0:T(8,128)(2,1)} %all-gather.3.cloned.1.call-done), kind=kOutput, calls=%fused_computation | convolution fusion | flops 2417491968 | bytes 7077888 | tf_op jit(solution)/shard_map/dot_general | solution.py:513
  63.9 32.2 %all-to-all-start = ((bf16[8,80,768]{2,1,0:T(8,128)(2,1)}), bf16[8,80,768]{2,1,0:T(8,128)(2,1)S(1)}, u32[]{:S(2)}, u32[]{:S(2)}) async-start(bf16[8,80,768]{2,1,0:T(8,128)(2,1)} %bitcast.212), calls=%async_computation | async-start | bytes 1966080 | tf_op jit(solution)/shard_map/all_to_all | solution.py:488
  96.7 7.4 %skew_bias.1.skew_ref = bf16[12,1920,128]{2,1,0:T(8,128)(2,1)} custom-call(f32[12,1,2048]{2,1,0:T(1,128)S(1)} %reshape.434.offset_ref), custom_call_target="tpu_custom_call" | custom-call | tf_op jit(solution)/shard_map/skew_bias/pallas_call | solution.py:43
  104.2 8.5 %collective-permute-start.12 = (bf16[768,768]{1,0:T(8,128)(2,1)}, bf16[768,768]{1,0:T(8,128)(2,1)}, u32[]{:S(2)}, u32[]{:S(2)}) collective-permute-start(bf16[768,768]{1,0:T(8,128)(2,1)} %bitcast.229), channel_id=1, source_target_pairs={{0,16},{8,24},{16,0},{24,8},{1,17},{9,25},{17,1},{25,9},{2,18},{10... | collective-permute-start | bytes 3538952 | tf_op jit(solution)/shard_map/ppermute | solution.py:342
  116.8 20.7 %attend_forward.1 = (f32[512,768]{1,0:T(8,128)S(1)}, f32[6,2,512]{2,1,0:T(2,128)S(1)}) custom-call(s32[2]{0:T(128)S(1)} %pad_add_fusion.1.base_ref, bf16[512,768]{1,0:T(8,128)(2,1)S(1)} %fusion.46.q_ref, bf16[1024,1536]{1,0:T(8,128)(2,1)} %convolution_convert_fusion.k_ref.v_ref, bf16[1024,1536]{1,0:T(8,128)(2,1)} %convolution_convert_fusion.k_ref.v_ref, ...), custom_call_target="tpu_custom_call" | custom-call | tf_op jit(solution)/shard_map/attend_forward/pallas_call | solution.py:107
  143.8 4.4 all-to-all-start.1
  148.7 16.4 %collective-permute-done.12 = bf16[768,768]{1,0:T(8,128)(2,1)} collective-permute-done((bf16[768,768]{1,0:T(8,128)(2,1)}, bf16[768,768]{1,0:T(8,128)(2,1)}, u32[]{:S(2)}, u32[]{:S(2)}) %collective-permute-start.12) | collective-permute-done | bytes 1179680 | tf_op jit(solution)/shard_map/ppermute | solution.py:342
  165.1 19.0 %collective-permute-done.11 = bf16[640,768]{1,0:T(8,128)(2,1)} collective-permute-done((bf16[640,768]{1,0:T(8,128)(2,1)S(1)}, bf16[640,768]{1,0:T(8,128)(2,1)}, u32[]{:S(2)}, u32[]{:S(2)}) %collective-permute-start.11) | collective-permute-done | bytes 983072 | tf_op jit(solution)/shard_map/ppermute | solution.py:342
  193.5 13.6 %collective-permute-done.13 = bf16[640,768]{1,0:T(8,128)(2,1)S(1)} collective-permute-done((bf16[640,768]{1,0:T(8,128)(2,1)S(1)}, bf16[640,768]{1,0:T(8,128)(2,1)S(1)}, u32[]{:S(2)}, u32[]{:S(2)}) %collective-permute-start.13) | collective-permute-done | bytes 983072 | tf_op jit(solution)/shard_map/ppermute | solution.py:342
  227.1 5.5 %fusion.4 = (bf16[640,768]{1,0:T(8,128)(2,1)}, f32[640]{0:T(1024)S(1)}, f32[640,768]{1,0:T(8,128)}) fusion(f32[640]{0:T(1024)S(1)} %get-tuple-element.84, bf16[8,80,768]{2,1,0:T(8,128)(2,1)S(1)} %all-to-all-done, f32[640,768]{1,0:T(8,128)S(1)} %copy-done.60, bf16[768,768]{1,0:T(8,128)(2,1)} %collective-permute-done.12, f32[640,768]{1,0:T(8,128)S(1)} %copy-done.58), kind=kOutput, calls=%fused_computation.27 | convolution fusion | flops 762346880 | bytes 9049088 | tf_op jit(solution)/shard_map/dot_general | solution.py:553
  261.9 4.7 collective-permute-done.14
  273.8 4.9 fusion.144
  283.2 6.4 %collective-permute-start.22 = (bf16[768,768]{1,0:T(8,128)(2,1)}, bf16[768,768]{1,0:T(8,128)(2,1)}, u32[]{:S(2)}, u32[]{:S(2)}) collective-permute-start(bf16[768,768]{1,0:T(8,128)(2,1)} %add_convert_fusion.1), channel_id=1, source_target_pairs={{0,16},{8,24},{16,0},{24,8},{1,17},{9,25},{17,1},{25,9},{2,18},{10... | collective-permute-start | bytes 3538952 | tf_op jit(solution)/shard_map/ppermute | solution.py:342
  293.1 27.3 %attend_backward.1 = (bf16[512,768]{1,0:T(8,128)(2,1)S(1)}, bf16[1024,768]{1,0:T(8,128)(2,1)S(1)}, bf16[1024,768]{1,0:T(8,128)(2,1)}, f32[6,2,2048]{2,1,0:T(2,128)S(1)}) custom-call(s32[2]{0:T(128)S(1)} %pad_add_fusion.1.base_ref, bf16[512,768]{1,0:T(8,128)(2,1)S(1)} %fusion.46.q_ref, bf16[512,768]{1,0:T(8,128)(2,1)S(1)} %convolution_convert_fusion.6.do_ref, ...), custom_call_target="tpu_custom_call" | custom-call | tf_op jit(solution)/shard_map/attend_backward/pallas_call | solution.py:205
  354.8 5.2 %multiply_reduce_fusion.2 = (f32[512]{0:T(512)S(1)}, f32[768]{0:T(1024)S(1)}, f32[512,768]{1,0:T(8,128)}) fusion(f32[1024,768]{1,0:T(8,128)} %maximum_convert_fusion, f32[512]{0:T(512)S(1)} %slice.72, f32[768]{0:T(1024)S(1)} %reshape.455, bf16[512,768]{1,0:T(8,128)(2,1)S(1)} %collective-permute-done.31, f32[1024,768]{1,0:T(8,128)} %copy-done.16, ...), kind=kOutput, calls=%fused_computation.79 | convolution fusion | flops 607517440 | bytes 9054208 | tf_op jit(solution)/shard_map/dot_general | solution.py:21
  380.6 8.9 %collective-permute-done.20 = bf16[96,2304]{1,0:T(8,128)(2,1)S(1)} collective-permute-done((bf16[96,2304]{1,0:T(8,128)(2,1)S(1)}, bf16[96,2304]{1,0:T(8,128)(2,1)S(1)}, u32[]{:S(2)}, u32[]{:S(2)}) %collective-permute-start.20) | collective-permute-done | bytes 442400 | tf_op jit(solution)/shard_map/ppermute | solution.py:342
  389.4 8.8 %collective-permute-done.19 = bf16[96,2304]{1,0:T(8,128)(2,1)S(1)} collective-permute-done((bf16[96,2304]{1,0:T(8,128)(2,1)S(1)}, bf16[96,2304]{1,0:T(8,128)(2,1)S(1)}, u32[]{:S(2)}, u32[]{:S(2)}) %collective-permute-start.19) | collective-permute-done | bytes 442400 | tf_op jit(solution)/shard_map/ppermute | solution.py:342
  403.8 7.9 %collective-permute-done.26 = bf16[24,2304]{1,0:T(8,128)(2,1)S(1)} collective-permute-done((bf16[24,2304]{1,0:T(8,128)(2,1)S(1)}, bf16[24,2304]{1,0:T(8,128)(2,1)S(1)}, u32[]{:S(2)}, u32[]{:S(2)}) %collective-permute-start.26) | collective-permute-done | bytes 110624 | tf_op jit(solution)/shard_map/ppermute | solution.py:342
  413.2 8.0 %collective-permute-done.25 = bf16[24,2304]{1,0:T(8,128)(2,1)S(1)} collective-permute-done((bf16[24,2304]{1,0:T(8,128)(2,1)S(1)}, bf16[24,2304]{1,0:T(8,128)(2,1)S(1)}, u32[]{:S(2)}, u32[]{:S(2)}) %collective-permute-start.25) | collective-permute-done | bytes 110624 | tf_op jit(solution)/shard_map/ppermute | solution.py:342
  432.9 4.7 add_bitcast_fusion
  439.7 5.5 %collective-permute-start.35 = (bf16[24,2304]{1,0:T(8,128)(2,1)S(1)}, bf16[24,2304]{1,0:T(8,128)(2,1)S(1)}, u32[]{:S(2)}, u32[]{:S(2)}) collective-permute-start(bf16[24,2304]{1,0:T(8,128)(2,1)S(1)} %fusion.95), channel_id=1, source_target_pairs={{0,24},{8,16},{16,8},{24,0},{1,25},{9,17},{17,9},{25,1},{2,26},{10... | collective-permute-start | bytes 331784 | tf_op jit(solution)/shard_map/ppermute | solution.py:342
  445.9 13.3 %collective-permute-done.35 = bf16[24,2304]{1,0:T(8,128)(2,1)S(1)} collective-permute-done((bf16[24,2304]{1,0:T(8,128)(2,1)S(1)}, bf16[24,2304]{1,0:T(8,128)(2,1)S(1)}, u32[]{:S(2)}, u32[]{:S(2)}) %collective-permute-start.35) | collective-permute-done | bytes 110624 | tf_op jit(solution)/shard_map/ppermute | solution.py:342
  459.2 10.2 %collective-permute-done.34 = bf16[24,2304]{1,0:T(8,128)(2,1)S(1)} collective-permute-done((bf16[24,2304]{1,0:T(8,128)(2,1)S(1)}, bf16[24,2304]{1,0:T(8,128)(2,1)S(1)}, u32[]{:S(2)}, u32[]{:S(2)}) %collective-permute-start.34) | collective-permute-done | bytes 110624 | tf_op jit(solution)/shard_map/ppermute | solution.py:342
  (361 shorter events, 207.3 us)
Async XLA Ops:
  7.2 48.6 %all-gather.3.cloned.1.call-start = ((), (), s32[]{:S(2)}) async-start(), calls=%async_computation.4 | async-start | bytes 3981312 | tf_op jit(solution)/shard_map/all_gather | solution.py:442
  8.0 130.1 %all-gather.5.cloned.1.call-start = ((), (), s32[]{:S(2)}) async-start(), calls=%async_computation.5 | async-start | bytes 1327104 | tf_op jit(solution)/shard_map/all_gather | solution.py:443
  9.2 20.5 %collective-permute-start = (bf16[256,768]{1,0:T(8,128)(2,1)S(1)}, bf16[256,768]{1,0:T(8,128)(2,1)S(1)}, u32[]{:S(2)}, u32[]{:S(2)}) collective-permute-start(bf16[256,768]{1,0:T(8,128)(2,1)S(1)} %get-tuple-element.109), channel_id=1, source_target_pairs={{0,0},{1,16},{2,2},{3,18},{4,4},{5,20},{6,6},{7,22},{8,8},{9,24},{... | collective-permute-start | bytes 1179656 | tf_op jit(solution)/shard_map/ppermute | solution.py:291
  19.0 31.6 %collective-permute-start.8 = (bf16[256,768]{1,0:T(8,128)(2,1)S(1)}, bf16[256,768]{1,0:T(8,128)(2,1)S(1)}, u32[]{:S(2)}, u32[]{:S(2)}) collective-permute-start(bf16[256,768]{1,0:T(8,128)(2,1)S(1)} %get-tuple-element.105), channel_id=1, source_target_pairs={{0,0},{1,16},{2,2},{3,18},{4,4},{5,20},{6,6},{7,22},{8,8},{9,24},{... | collective-permute-start | bytes 1179656 | tf_op jit(solution)/shard_map/ppermute | solution.py:291
  21.8 28.8 %collective-permute-start.9 = (bf16[256,768]{1,0:T(8,128)(2,1)S(1)}, bf16[256,768]{1,0:T(8,128)(2,1)}, u32[]{:S(2)}, u32[]{:S(2)}) collective-permute-start(bf16[256,768]{1,0:T(8,128)(2,1)S(1)} %get-tuple-element.106), channel_id=1, source_target_pairs={{0,8},{1,24},{2,10},{3,26},{4,12},{5,28},{6,14},{7,30},{8,0},{9,16... | collective-permute-start | bytes 1179656 | tf_op jit(solution)/shard_map/ppermute | solution.py:291
  29.9 23.5 %collective-permute-start.2 = (bf16[512,768]{1,0:T(8,128)(2,1)S(1)}, bf16[512,768]{1,0:T(8,128)(2,1)S(1)}, u32[]{:S(2)}, u32[]{:S(2)}) collective-permute-start(bf16[512,768]{1,0:T(8,128)(2,1)S(1)} %pad_maximum_fusion.2), channel_id=1, source_target_pairs={{0,1},{1,0},{2,3},{3,2},{4,5},{5,4},{6,7},{7,6},{8,9},{9,8},{10,11... | collective-permute-start | bytes 2359304 | tf_op jit(solution)/shard_map/ppermute | solution.py:321
  46.6 91.5 %collective-permute-start.10 = (bf16[768,768]{1,0:T(8,128)(2,1)}, bf16[768,768]{1,0:T(8,128)(2,1)}, u32[]{:S(2)}, u32[]{:S(2)}) collective-permute-start(bf16[768,768]{1,0:T(8,128)(2,1)} %bitcast.230), channel_id=1, source_target_pairs={{0,16},{8,24},{16,0},{24,8},{1,17},{9,25},{17,1},{25,9},{2,18},{10... | collective-permute-start | bytes 3538952 | tf_op jit(solution)/shard_map/ppermute | solution.py:342
  63.9 73.5 %all-to-all-start = ((bf16[8,80,768]{2,1,0:T(8,128)(2,1)}), bf16[8,80,768]{2,1,0:T(8,128)(2,1)S(1)}, u32[]{:S(2)}, u32[]{:S(2)}) async-start(bf16[8,80,768]{2,1,0:T(8,128)(2,1)} %bitcast.212), calls=%async_computation | async-start | bytes 1966080 | tf_op jit(solution)/shard_map/all_to_all | solution.py:488
  104.2 60.9 %collective-permute-start.12 = (bf16[768,768]{1,0:T(8,128)(2,1)}, bf16[768,768]{1,0:T(8,128)(2,1)}, u32[]{:S(2)}, u32[]{:S(2)}) collective-permute-start(bf16[768,768]{1,0:T(8,128)(2,1)} %bitcast.229), channel_id=1, source_target_pairs={{0,16},{8,24},{16,0},{24,8},{1,17},{9,25},{17,1},{25,9},{2,18},{10... | collective-permute-start | bytes 3538952 | tf_op jit(solution)/shard_map/ppermute | solution.py:342
  137.4 46.6 %collective-permute-start.11 = (bf16[640,768]{1,0:T(8,128)(2,1)S(1)}, bf16[640,768]{1,0:T(8,128)(2,1)}, u32[]{:S(2)}, u32[]{:S(2)}) collective-permute-start(bf16[640,768]{1,0:T(8,128)(2,1)S(1)} %bitcast.207), channel_id=1, source_target_pairs={{0,8},{8,0},{16,24},{24,16},{1,9},{9,1},{17,25},{25,17},{2,10},{10... | collective-permute-start | bytes 2949128 | tf_op jit(solution)/shard_map/ppermute | solution.py:342
  143.8 21.2 %all-to-all-start.1 = ((bf16[8,80,768]{2,1,0:T(8,128)(2,1)}), bf16[8,80,768]{2,1,0:T(8,128)(2,1)S(1)}, u32[]{:S(2)}, u32[]{:S(2)}) async-start(bf16[8,80,768]{2,1,0:T(8,128)(2,1)} %bitcast.211), calls=%async_computation.1 | async-start | bytes 1966080 | tf_op jit(solution)/shard_map/all_to_all | solution.py:488
  184.1 23.1 %collective-permute-start.13 = (bf16[640,768]{1,0:T(8,128)(2,1)S(1)}, bf16[640,768]{1,0:T(8,128)(2,1)S(1)}, u32[]{:S(2)}, u32[]{:S(2)}) collective-permute-start(bf16[640,768]{1,0:T(8,128)(2,1)S(1)} %bitcast.198), channel_id=1, source_target_pairs={{0,8},{8,0},{16,24},{24,16},{1,9},{9,1},{17,25},{25,17},{2,10},{10... | collective-permute-start | bytes 2949128 | tf_op jit(solution)/shard_map/ppermute | solution.py:342
  244.2 22.5 %collective-permute-start.14 = (bf16[640,768]{1,0:T(8,128)(2,1)}, bf16[640,768]{1,0:T(8,128)(2,1)}, u32[]{:S(2)}, u32[]{:S(2)}) collective-permute-start(bf16[640,768]{1,0:T(8,128)(2,1)} %add_convert_fusion.4), channel_id=1, source_target_pairs={{0,8},{8,0},{16,24},{24,16},{1,9},{9,1},{17,25},{25,17},{2,10},{10... | collective-permute-start | bytes 2949128 | tf_op jit(solution)/shard_map/ppermute | solution.py:342
  282.5 45.5 %collective-permute-start.15 = (bf16[640,768]{1,0:T(8,128)(2,1)}, bf16[640,768]{1,0:T(8,128)(2,1)}, u32[]{:S(2)}, u32[]{:S(2)}) collective-permute-start(bf16[640,768]{1,0:T(8,128)(2,1)} %get-tuple-element.48), channel_id=1, source_target_pairs={{0,8},{8,0},{16,24},{24,16},{1,9},{9,1},{17,25},{25,17},{2,10},{10... | collective-permute-start | bytes 2949128 | tf_op jit(solution)/shard_map/ppermute | solution.py:342
  283.2 116.1 %collective-permute-start.22 = (bf16[768,768]{1,0:T(8,128)(2,1)}, bf16[768,768]{1,0:T(8,128)(2,1)}, u32[]{:S(2)}, u32[]{:S(2)}) collective-permute-start(bf16[768,768]{1,0:T(8,128)(2,1)} %add_convert_fusion.1), channel_id=1, source_target_pairs={{0,16},{8,24},{16,0},{24,8},{1,17},{9,25},{17,1},{25,9},{2,18},{10... | collective-permute-start | bytes 3538952 | tf_op jit(solution)/shard_map/ppermute | solution.py:342
  289.5 109.7 %collective-permute-start.23 = (bf16[768,768]{1,0:T(8,128)(2,1)}, bf16[768,768]{1,0:T(8,128)(2,1)}, u32[]{:S(2)}, u32[]{:S(2)}) collective-permute-start(bf16[768,768]{1,0:T(8,128)(2,1)} %add_convert_fusion), channel_id=1, source_target_pairs={{0,16},{8,24},{16,0},{24,8},{1,17},{9,25},{17,1},{25,9},{2,18},{10... | collective-permute-start | bytes 3538952 | tf_op jit(solution)/shard_map/ppermute | solution.py:342
  350.0 23.4 %collective-permute-start.17 = (bf16[4,96,2304]{2,1,0:T(8,128)(2,1)}, bf16[4,96,2304]{2,1,0:T(8,128)(2,1)}, u32[]{:S(2)}, u32[]{:S(2)}) collective-permute-start(bf16[4,96,2304]{2,1,0:T(8,128)(2,1)} %dynamic-slice_bitcast_fusion), channel_id=1, source_target_pairs={{0,1},{1,0},{2,3},{3,2},{4,5},{5,4},{6,7},{7,6},{8,9},{9,8},{10,11... | collective-permute-start | bytes 5308424 | tf_op jit(solution)/shard_map/ppermute | solution.py:342
  378.7 20.3 %collective-permute-start.18 = (bf16[96,2304]{1,0:T(8,128)(2,1)S(1)}, bf16[96,2304]{1,0:T(8,128)(2,1)S(1)}, u32[]{:S(2)}, u32[]{:S(2)}) collective-permute-start(bf16[96,2304]{1,0:T(8,128)(2,1)S(1)} %get-tuple-element.88), channel_id=1, source_target_pairs={{0,2},{1,3},{2,0},{3,1},{4,6},{5,7},{6,4},{7,5},{8,10},{9,11},{10,... | collective-permute-start | bytes 1327112 | tf_op jit(solution)/shard_map/ppermute | solution.py:342
  389.4 48.1 %collective-permute-start.30 = (bf16[256,768]{1,0:T(8,128)(2,1)S(1)}, bf16[256,768]{1,0:T(8,128)(2,1)S(1)}, u32[]{:S(2)}, u32[]{:S(2)}) collective-permute-start(bf16[256,768]{1,0:T(8,128)(2,1)S(1)} %get-tuple-element.102), channel_id=1, source_target_pairs={{8,0},{24,1},{10,2},{26,3},{12,4},{28,5},{14,6},{30,7},{0,8},{16,9... | collective-permute-start | bytes 1179656 | tf_op jit(solution)/shard_map/ppermute | solution.py:305
  398.3 39.9 %collective-permute-start.16 = (bf16[256,768]{1,0:T(8,128)(2,1)S(1)}, bf16[256,768]{1,0:T(8,128)(2,1)S(1)}, u32[]{:S(2)}, u32[]{:S(2)}) collective-permute-start(bf16[256,768]{1,0:T(8,128)(2,1)S(1)} %get-tuple-element.101), channel_id=1, source_target_pairs={{0,0},{16,1},{2,2},{18,3},{4,4},{20,5},{6,6},{22,7},{8,8},{24,9},{... | collective-permute-start | bytes 1179656 | tf_op jit(solution)/shard_map/ppermute | solution.py:305
  437.5 36.5 %collective-permute-start.32 = (bf16[256,768]{1,0:T(8,128)(2,1)S(1)}, bf16[256,768]{1,0:T(8,128)(2,1)S(1)}, u32[]{:S(2)}, u32[]{:S(2)}) collective-permute-start(bf16[256,768]{1,0:T(8,128)(2,1)S(1)} %get-tuple-element.97), channel_id=1, source_target_pairs={{0,0},{16,1},{2,2},{18,3},{4,4},{20,5},{6,6},{22,7},{8,8},{24,9},{... | collective-permute-start | bytes 1179656 | tf_op jit(solution)/shard_map/ppermute | solution.py:305
  438.2 36.5 %collective-permute-start.39 = (bf16[256,768]{1,0:T(8,128)(2,1)S(1)}, bf16[256,768]{1,0:T(8,128)(2,1)S(1)}, u32[]{:S(2)}, u32[]{:S(2)}) collective-permute-start(bf16[256,768]{1,0:T(8,128)(2,1)S(1)} %get-tuple-element.98), channel_id=1, source_target_pairs={{8,0},{24,1},{10,2},{26,3},{12,4},{28,5},{14,6},{30,7},{0,8},{16,9... | collective-permute-start | bytes 1179656 | tf_op jit(solution)/shard_map/ppermute | solution.py:305
  445.2 24.2 %collective-permute-start.34 = (bf16[24,2304]{1,0:T(8,128)(2,1)S(1)}, bf16[24,2304]{1,0:T(8,128)(2,1)S(1)}, u32[]{:S(2)}, u32[]{:S(2)}) collective-permute-start(bf16[24,2304]{1,0:T(8,128)(2,1)S(1)} %fusion.95), channel_id=1, source_target_pairs={{0,16},{8,24},{16,0},{24,8},{1,17},{9,25},{17,1},{25,9},{2,18},{10... | collective-permute-start | bytes 331784 | tf_op jit(solution)/shard_map/ppermute | solution.py:342
  445.2 24.2 %collective-permute-start.33 = (bf16[24,2304]{1,0:T(8,128)(2,1)S(1)}, bf16[24,2304]{1,0:T(8,128)(2,1)S(1)}, u32[]{:S(2)}, u32[]{:S(2)}) collective-permute-start(bf16[24,2304]{1,0:T(8,128)(2,1)S(1)} %fusion.95), channel_id=1, source_target_pairs={{0,8},{8,0},{16,24},{24,16},{1,9},{9,1},{17,25},{25,17},{2,10},{10... | collective-permute-start | bytes 331784 | tf_op jit(solution)/shard_map/ppermute | solution.py:342
  (93 other events, 1030.2 us)
Sparse Core Ops, SparseCore 0:
  10.0 37.6 all-gather.2
  49.5 23.2 all-gather.4
